TPU v7x, 256 devices: a whole 4x4x8 slice. The times are simulated.
256 devices in a mesh: dp: 4 (over x_lo, core), axial: 64 (over y, z, x_hi).
Axes of the slice: x: 4 (x_hi: 2, x_lo: 2; x = x_hi * 2 + x_lo), y: 4, z: 8, core: 2. Of those that a mesh axis runs over, the one named last changes fastest.
Arguments:
- homolog_matrix: bfloat16 [4, 512, 256, 256], P('dp', 'axial'), may hold values from -6 to 6
- couple_matrix: bfloat16 [4, 256, 256, 128], P('dp', 'axial'), may hold values from -8 to 8
- result_adjoint: bfloat16 [4, 512, 256, 256], P('dp', 'axial'), may hold values from -16 to 16
- joint_projection_matrix: bfloat16 [256, 1024], replicated, may hold values from -0.375 to 0.375
- sigmoid_shift_vector: float32 [256], replicated, may hold values from -4 to 4
- final_projection_matrix: bfloat16 [256, 256], replicated, may hold values from -0.375 to 0.375
- homolog_standardize_multiplier: float32 [256], replicated, may hold values from 0.25 to 1.75
- homolog_standardize_shift: float32 [256], replicated, may hold values from -3 to 3
- couple_standardize_multiplier: float32 [128], replicated, may hold values from 0.25 to 1.75
- couple_headshift_matrix: bfloat16 [128, 8], replicated, may hold values from -4 to 4
Outputs:
- homolog_matrix_derivative: bfloat16 [4, 512, 256, 256], P('dp', 'axial')
- couple_matrix_derivative: bfloat16 [4, 256, 256, 128], P('dp', 'axial')
- d_w_qkvg: float32 [256, 1024], replicated
- d_g_bias: float32 [256], replicated
- d_w_out: float32 [256, 256], replicated
- d_msa_gain: float32 [256], replicated
- d_msa_beta: float32 [256], replicated
- d_pair_gain: float32 [128], replicated
- d_w_bias: float32 [128, 8], replicated
All inputs are finite; a program needn't handle non-finite values.
Results may differ from a plain program's by a relative error of at most 0.017.
The roundings to bfloat16 on the way count: a program that leaves them out, or rounds other values in their place, can miss the bound.
Values may be sent and summed in bfloat16 or wider, within the bound.
No kernel may reach another device: no remote copies, remote signals or barrier semaphores. Data moves between devices by JAX's collectives and lax.ppermute only.
A program may use at most 64 MiB of HBM per device.

v0:
```python
import jax
import jax.numpy as jnp
from jax import lax
from jax.sharding import PartitionSpec as P

eps_norm = 1e-05


def apply_layer_norm(values):
    average = jnp.mean(values, axis=-1, keepdims=True)
    centered = values - average
    inverse_deviation = lax.rsqrt(jnp.mean(centered * centered, axis=-1, keepdims=True) + eps_norm)
    return (centered * inverse_deviation, inverse_deviation)


def layer_norm_reverse(grad_unit, normalized_rows, inverse_deviation):
    grad_mean = jnp.mean(grad_unit, axis=-1, keepdims=True)
    cross_mean = jnp.mean(grad_unit * normalized_rows, axis=-1, keepdims=True)
    return inverse_deviation * (grad_unit - grad_mean - normalized_rows * cross_mean)


def pair_normed(pair_rows, couple_standardize_multiplier):
    normalized_rows, inverse_deviation = apply_layer_norm(pair_rows.astype(jnp.float32))
    normalized_input = (normalized_rows * couple_standardize_multiplier).astype(jnp.bfloat16)
    return (normalized_input, normalized_rows, inverse_deviation)


def pair_project(normalized_input, couple_headshift_matrix):
    return jnp.einsum(
        "ijc,ch->hij", normalized_input, couple_headshift_matrix, preferred_element_type=jnp.float32
    )


def pair_backward(
    bias_gradient,
    normalized_input,
    normalized_rows,
    inverse_deviation,
    couple_standardize_multiplier,
    couple_headshift_matrix,
):
    d_pnormed = jnp.einsum(
        "hij,ch->ijc", bias_gradient, couple_headshift_matrix.astype(jnp.float32)
    )
    d_wbias = jnp.einsum("ijc,hij->ch", normalized_input.astype(jnp.float32), bias_gradient)
    d_pgain = jnp.sum(normalized_rows * d_pnormed, axis=(0, 1))
    couple_matrix_derivative = layer_norm_reverse(
        d_pnormed * couple_standardize_multiplier, normalized_rows, inverse_deviation
    ).astype(jnp.bfloat16)
    return (couple_matrix_derivative, d_wbias, d_pgain)


def per_row_gradients(
    alignment_row,
    row_output_gradient,
    complete_bias,
    homolog_standardize_multiplier,
    homolog_standardize_shift,
    joint_projection_matrix,
    sigmoid_shift_vector,
    final_projection_matrix,
):
    residue_total = alignment_row.shape[0]
    head_width = final_projection_matrix.shape[0]
    num_heads = complete_bias.shape[0]
    head_size = head_width // num_heads
    factor = head_size ** (-0.5)
    single_precision = jnp.float32
    normalized_rows, inverse_deviation = apply_layer_norm(alignment_row.astype(single_precision))
    normalized_input = (
        normalized_rows * homolog_standardize_multiplier + homolog_standardize_shift
    ).astype(jnp.bfloat16)
    projected = jnp.dot(
        normalized_input, joint_projection_matrix, preferred_element_type=single_precision
    )
    queries = (
        (projected[:, :head_width] * factor)
        .astype(jnp.bfloat16)
        .reshape(residue_total, num_heads, head_size)
    )
    key_rows = (
        projected[:, head_width : 2 * head_width]
        .astype(jnp.bfloat16)
        .reshape(residue_total, num_heads, head_size)
    )
    value_rows = (
        projected[:, 2 * head_width : 3 * head_width]
        .astype(jnp.bfloat16)
        .reshape(residue_total, num_heads, head_size)
    )
    gating = jax.nn.sigmoid(projected[:, 3 * head_width :] + sigmoid_shift_vector)
    logits = (
        jnp.einsum("ihd,jhd->hij", queries, key_rows, preferred_element_type=single_precision)
        + complete_bias
    )
    attn = jax.nn.softmax(logits, axis=-1)
    attn_low = attn.astype(jnp.bfloat16)
    attended = jnp.einsum(
        "hij,jhd->ihd", attn_low, value_rows, preferred_element_type=single_precision
    ).reshape(residue_total, head_width)
    gated = (gating * attended).astype(jnp.bfloat16)
    d_gated = jnp.dot(
        row_output_gradient, final_projection_matrix.T, preferred_element_type=single_precision
    )
    d_wout = jnp.dot(gated.T, row_output_gradient, preferred_element_type=single_precision)
    d_attended = (
        (d_gated * gating).astype(jnp.bfloat16).reshape(residue_total, num_heads, head_size)
    )
    d_graw = d_gated * attended * gating * (1.0 - gating)
    d_attn = jnp.einsum(
        "ihd,jhd->hij", d_attended, value_rows, preferred_element_type=single_precision
    )
    d_values = jnp.einsum(
        "hij,ihd->jhd", attn_low, d_attended, preferred_element_type=single_precision
    )
    logit_gradient = attn * (d_attn - jnp.sum(attn * d_attn, axis=-1, keepdims=True))
    d_low = logit_gradient.astype(jnp.bfloat16)
    d_queries = (
        jnp.einsum("hij,jhd->ihd", d_low, key_rows, preferred_element_type=single_precision)
        * factor
    )
    d_keys = jnp.einsum("hij,ihd->jhd", d_low, queries, preferred_element_type=single_precision)
    d_projected = jnp.concatenate(
        [
            d_queries.reshape(residue_total, head_width),
            d_keys.reshape(residue_total, head_width),
            d_values.reshape(residue_total, head_width),
            d_graw,
        ],
        axis=1,
    ).astype(jnp.bfloat16)
    d_wqkvg = jnp.dot(normalized_input.T, d_projected, preferred_element_type=single_precision)
    normalized_gradient = jnp.dot(
        d_projected, joint_projection_matrix.T, preferred_element_type=single_precision
    )
    alignment_row_gradient = layer_norm_reverse(
        normalized_gradient * homolog_standardize_multiplier, normalized_rows, inverse_deviation
    ).astype(jnp.bfloat16)
    gradient_tree = (
        d_wqkvg,
        jnp.sum(d_graw, axis=0),
        d_wout,
        jnp.sum(normalized_rows * normalized_gradient, axis=0),
        jnp.sum(normalized_gradient, axis=0),
    )
    return (alignment_row_gradient, logit_gradient, gradient_tree)


def local(
    homolog_matrix,
    couple_matrix,
    result_adjoint,
    joint_projection_matrix,
    sigmoid_shift_vector,
    final_projection_matrix,
    homolog_standardize_multiplier,
    homolog_standardize_shift,
    couple_standardize_multiplier,
    couple_headshift_matrix,
):
    single_precision = jnp.float32
    normalized_input, normalized_rows, inverse_deviation = pair_normed(
        couple_matrix[0], couple_standardize_multiplier
    )
    own_bias = pair_project(normalized_input, couple_headshift_matrix)[None]
    complete_bias = lax.all_gather(own_bias, "axial", axis=2, tiled=True)[0]

    def per_row_update(running, partial_results):
        single_row_gradient, logit_gradient, gradient_tree = per_row_gradients(
            partial_results[0],
            partial_results[1],
            complete_bias,
            homolog_standardize_multiplier,
            homolog_standardize_shift,
            joint_projection_matrix,
            sigmoid_shift_vector,
            final_projection_matrix,
        )
        return (
            (running[0] + logit_gradient, jax.tree.map(jnp.add, running[1], gradient_tree)),
            single_row_gradient,
        )

    initial_gradients = (
        jnp.zeros(joint_projection_matrix.shape, single_precision),
        jnp.zeros(sigmoid_shift_vector.shape, single_precision),
        jnp.zeros(final_projection_matrix.shape, single_precision),
        jnp.zeros(homolog_standardize_multiplier.shape, single_precision),
        jnp.zeros(homolog_standardize_multiplier.shape, single_precision),
    )
    (bias_gradient, gradient_tree), stacked_row_gradients = lax.scan(
        per_row_update,
        (jnp.zeros(complete_bias.shape, single_precision), initial_gradients),
        (homolog_matrix[0], result_adjoint[0]),
    )
    d_local = lax.psum_scatter(bias_gradient[None], "axial", scatter_dimension=2, tiled=True)[0]
    couple_matrix_derivative, d_wbias, d_pgain = pair_backward(
        d_local,
        normalized_input,
        normalized_rows,
        inverse_deviation,
        couple_standardize_multiplier,
        couple_headshift_matrix,
    )
    reduced_sum = lax.psum(
        (
            gradient_tree[0],
            gradient_tree[1],
            gradient_tree[2],
            gradient_tree[3],
            gradient_tree[4],
            d_wbias,
            d_pgain,
        ),
        ("dp", "axial"),
    )
    window_group = lax.axis_size("dp") * homolog_matrix.shape[0]
    homolog_multiplier_term = float(
        window_group * homolog_matrix.shape[1] * lax.axis_size("axial") * homolog_matrix.shape[2]
    ) ** (-0.5)
    pairwise_scale_factor = float(
        window_group * couple_matrix.shape[1] * lax.axis_size("axial") * couple_matrix.shape[2]
    ) ** (-0.5)
    return (
        stacked_row_gradients[None],
        couple_matrix_derivative[None],
        reduced_sum[0] * homolog_multiplier_term,
        reduced_sum[1] * homolog_multiplier_term,
        reduced_sum[2] * homolog_multiplier_term,
        reduced_sum[3] * homolog_multiplier_term,
        reduced_sum[4] * homolog_multiplier_term,
        reduced_sum[6] * pairwise_scale_factor,
        reduced_sum[5] * pairwise_scale_factor,
    )


def solution(mesh):
    placed = (
        P("dp", "axial", None, None),
        P("dp", "axial", None, None),
        P("dp", "axial", None, None),
        P(),
        P(),
        P(),
        P(),
        P(),
        P(),
        P(),
    )
    return jax.shard_map(
        local,
        mesh=mesh,
        in_specs=placed,
        out_specs=(
            P("dp", "axial", None, None),
            P("dp", "axial", None, None),
            P(),
            P(),
            P(),
            P(),
            P(),
            P(),
            P(),
        ),
        check_vma=False,
    )
```

profile of v0, /device:TPU:2, one launch (start us, length us, event | category | flops | bytes accessed | tf_op | source)
XLA Modules:
  0.0 1098.9 jit_solution(17794163005143551037)
XLA Ops:
  10.2 122.1 %all-gather.3.cloned.1.call-done = f32[8,256,256]{2,0,1:T(8,128)} async-done(((f32[8,4,256]{2,0,1:T(8,128)}), f32[8,256,256]{2,0,1:T(8,128)}) %all-gather.3.cloned.1.call-update) | async-done | bytes 2097168 | tf_op jit(solution)/shard_map/all_gather | solution.py:166
  132.3 1.9 copy.83
  134.2 257.3 %while.23 = (s32[]{:T(128)}, f32[8,256,256]{1,2,0:T(8,128)}, f32[256,1024]{1,0:T(8,128)}, f32[256]{0:T(256)}, f32[256,256]{1,0:T(8,128)}, /*index=5*/f32[256]{0:...) while((s32[]{:T(128)}, f32[8,256,256]{1,2,0:T(8,128)}, ...), condition=%wide.region_13.14_spmd.clone, body=%wide.region_2.13_spmd.clone.sunk | while | flops 689639168 | bytes 96337616 | solution.py:191
  139.6 1.6 fusion.160
  141.2 3.5 fusion.161
  144.7 1.8 copy.105
  146.5 2.0 convolution_add_fusion.8
  148.5 2.6 fusion.162
  152.1 2.8 convolution_convert_fusion.4
  163.6 2.0 fusion.166
  170.9 1.6 fusion.160
  172.6 3.5 fusion.161
  176.1 1.8 copy.105
  177.8 2.1 convolution_add_fusion.8
  179.9 2.6 fusion.162
  183.6 2.8 convolution_convert_fusion.4
  195.9 2.0 fusion.166
  203.2 1.6 fusion.160
  204.8 3.5 fusion.161
  208.3 1.8 copy.105
  210.1 2.1 convolution_add_fusion.8
  212.2 2.6 fusion.162
  215.8 2.8 convolution_convert_fusion.4
  228.1 2.0 fusion.166
  235.5 1.6 fusion.160
  237.1 3.5 fusion.161
  240.6 1.8 copy.105
  242.4 2.1 convolution_add_fusion.8
  244.5 2.6 fusion.162
  248.1 2.8 convolution_convert_fusion.4
  260.4 2.0 fusion.166
  267.8 1.6 fusion.160
  269.4 3.5 fusion.161
  272.9 1.8 copy.105
  274.7 2.1 convolution_add_fusion.8
  276.8 2.6 fusion.162
  280.4 2.8 convolution_convert_fusion.4
  292.7 2.0 fusion.166
  300.0 1.6 fusion.160
  301.7 3.5 fusion.161
  305.2 1.8 copy.105
  307.0 2.1 convolution_add_fusion.8
  309.0 2.6 fusion.162
  312.7 2.8 convolution_convert_fusion.4
  325.0 2.0 fusion.166
  332.3 1.6 fusion.160
  334.0 3.5 fusion.161
  337.4 1.8 copy.105
  339.2 2.1 convolution_add_fusion.8
  341.3 2.6 fusion.162
  345.0 2.8 convolution_convert_fusion.4
  357.3 2.0 fusion.166
  366.2 3.5 fusion.161
  369.7 1.8 copy.105
  371.5 2.1 convolution_add_fusion.8
  373.6 2.6 fusion.162
  377.2 2.8 convolution_convert_fusion.4
  389.5 2.0 fusion.166
  391.6 3.1 copy.84
  394.7 253.7 %all-reduce.4.cloned.1.call-done = (f32[256,1024]{1,0:T(8,128)}, f32[256,256]{1,0:T(8,128)}) async-done(((f32[256,1024]{1,0:T(8,128)}, f32[256,256]{1,0:T(8,128)}), (f32[256,1024]{1,0:T(8,128)}, f32[256,256]{1,0:T(8,128)})) %all-reduce.4.cloned.1.call-update) | async-done | bytes 1310736 | tf_op jit(solution)/shard_map/psum | solution.py:205
  648.5 1.7 broadcast_multiply_fusion.4
  650.2 2.3 broadcast_multiply_fusion.3
  652.5 362.8 %reduce-scatter.2.cloned.1.call-done = f32[1,8,4,256]{3,1,0,2:T(8,128)} async-done(((f32[1,8,256,256]{3,1,0,2:T(8,128)}), f32[1,8,4,256]{3,1,0,2:T(8,128)}) %reduce-scatter.2.cloned.1.call-update) | async-done | bytes 32784 | tf_op jit(solution)/shard_map/reduce_scatter | solution.py:196
  1017.6 71.5 %all-reduce = (f32[256]{0:T(256)S(1)}, f32[256]{0:T(256)S(1)}, f32[256]{0:T(256)S(1)}, f32[128]{0:T(128)S(1)}, f32[128,8]{0,1:T(8,128)S(1)}) all-reduce(f32[256]{0:T(256)S(1)} %copy-done.18, f32[256]{0:T(256)S(1)} %copy-done.22, f32[256]{0:T(256)S(1)} %copy-done.21, ...), channel_id=1, replica_groups=mesh['dp'=4,'axial'=64] {'dp','axial'}, use_global_device_ids=true, to_apply=%region_18.19 | all-reduce | flops 1920 | bytes 15360 | tf_op jit(solution)/shard_map/psum | solution.py:205
  (515 shorter events, 134.1 us)
Async XLA Ops:
  7.2 125.1 %all-gather.3.cloned.1.call-start = ((), (), s32[]{:S(2)}) async-start(), calls=%async_computation.2 | async-start | bytes 2129920 | tf_op jit(solution)/shard_map/all_gather | solution.py:166
  8.3 1.8 copy-start.7
  8.4 1.8 copy-start.14
  10.0 638.4 %all-reduce.4.cloned.1.call-start = ((), (), s32[]{:S(2)}) async-start(), calls=%async_computation.3 | async-start | bytes 2621440 | tf_op jit(solution)/shard_map/psum | solution.py:205
  134.2 4.8 copy-start.4
  152.1 2.9 copy-start.16
  152.1 2.9 copy-start.23
  159.2 2.9 copy-start.10
  160.9 4.7 copy-start.5
  163.6 2.0 copy-start.11
  165.6 4.8 copy-start.4
  183.5 2.9 copy-start.16
  183.6 2.9 copy-start.23
  190.6 1.7 copy-start.19
  190.6 3.7 copy-start.10
  192.3 5.5 copy-start.5
  195.9 2.0 copy-start.11
  197.9 4.8 copy-start.4
  215.8 2.9 copy-start.16
  215.8 2.9 copy-start.23
  222.9 3.7 copy-start.10
  224.6 5.5 copy-start.5
  228.1 2.0 copy-start.11
  230.1 4.8 copy-start.4
  248.1 2.9 copy-start.16
  248.1 2.9 copy-start.23
  255.2 1.7 copy-start.19
  255.2 3.7 copy-start.10
  256.9 5.5 copy-start.5
  260.4 2.0 copy-start.11
  262.4 4.8 copy-start.4
  280.4 2.9 copy-start.16
  280.4 2.9 copy-start.23
  287.5 3.7 copy-start.10
  289.2 5.5 copy-start.5
  292.7 2.0 copy-start.11
  294.7 4.8 copy-start.4
  312.7 2.9 copy-start.16
  312.7 2.9 copy-start.23
  319.7 1.7 copy-start.19
  319.7 3.7 copy-start.10
  321.5 5.5 copy-start.5
  325.0 2.0 copy-start.11
  327.0 4.8 copy-start.4
  344.9 2.9 copy-start.16
  345.0 2.9 copy-start.23
  352.0 3.7 copy-start.10
  353.7 5.5 copy-start.5
  357.2 2.0 copy-start.11
  359.2 4.8 copy-start.4
  377.2 2.9 copy-start.16
  377.2 2.9 copy-start.23
  384.3 1.7 copy-start.19
  384.3 3.7 copy-start.10
  386.0 5.5 copy-start.5
  389.5 2.0 copy-start.11
  391.6 623.8 %reduce-scatter.2.cloned.1.call-start = ((), (), s32[]{:S(2)}) async-start(), calls=%async_computation.1 | async-start | bytes 2129920 | tf_op jit(solution)/shard_map/reduce_scatter | solution.py:196
  394.7 620.6 %copy-start.8 = (bf16[1,4,256,128]{2,3,1,0:T(8,128)(2,1)S(1)}, bf16[1,4,256,128]{2,3,1,0:T(8,128)(2,1)}, u32[]{:S(2)}) copy-start(bf16[1,4,256,128]{2,3,1,0:T(8,128)(2,1)} %copy-done.7) | copy-start | bytes 786436
  394.7 620.6 %copy-start.15 = (f32[4,256]{1,0:T(4,128)S(1)}, f32[4,256]{1,0:T(4,128)}, u32[]{:S(2)}) copy-start(f32[4,256]{1,0:T(4,128)} %copy-done.14) | copy-start | bytes 12292
  394.7 620.7 %copy-start.25 = (f32[4,256]{1,0:T(4,128)S(1)}, f32[4,256]{1,0:T(4,128)}, u32[]{:S(2)}) copy-start(f32[4,256]{1,0:T(4,128)} %copy-done.24) | copy-start | bytes 12292
  394.7 620.7 %copy-start.26 = (f32[128]{0:T(128)S(1)}, f32[128]{0:T(128)}, u32[]{:S(2)}) copy-start(f32[128]{0:T(128)} %param.20) | copy-start | bytes 1540
  648.4 369.1 %copy-start.18 = (f32[256]{0:T(256)S(1)}, f32[256]{0:T(256)}, u32[]{:S(2)}) copy-start(f32[256]{0:T(256)} %get-tuple-element.100) | copy-start | bytes 3076
  648.4 369.1 %copy-start.21 = (f32[256]{0:T(256)S(1)}, f32[256]{0:T(256)}, u32[]{:S(2)}) copy-start(f32[256]{0:T(256)} %get-tuple-element.103) | copy-start | bytes 3076
  648.4 369.1 %copy-start.22 = (f32[256]{0:T(256)S(1)}, f32[256]{0:T(256)}, u32[]{:S(2)}) copy-start(f32[256]{0:T(256)} %get-tuple-element.102) | copy-start | bytes 3076
  (86 other events, 117.7 us)
Sparse Core Ops, SparseCore 0:
  11.6 120.6 all-gather.2
  391.7 256.7 all-reduce.3
  651.1 364.2 reduce-scatter.1
where the time goes:
time: 1100 us
  waiting for transfers between devices  739 us (67%)
  matrix products  140 us (13%)
  other arithmetic  73.8 us (7%)
  blocking collectives  71.5 us (6%)
  local copies, waits for them, and re-layouts  58 us (5%)
  between operations  14 us (1%)
    reduce_scatter x1, waiting for transfers between devices, local(): lax.psum_scatter(bias_gradient[None], 'axial', scatter_dimension=2, tiled...  363 us
    psum x1, waiting for transfers between devices, local(): lax.psum((gradient_tree[0], gradient_tree[1], gradient_tree[2], gradient_...  254 us
    all_gather x1, waiting for transfers between devices, local(): complete_bias = lax.all_gather(own_bias, 'axial', axis=2, tiled=True)[0]  122 us
    psum x1, blocking collectives, local(): lax.psum((gradient_tree[0], gradient_tree[1], gradient_tree[2], gradient_...  71.5 us
    dot_general x8, matrix products, per_row_gradients(): jnp.einsum('hij,jhd->ihd', attn_low, value_rows, preferred_element_type=s...  28 us
    dot_general x8, matrix products, per_row_gradients(): jnp.einsum('hij,ihd->jhd', attn_low, d_attended, preferred_element_type=s...  22.2 us
  transfers between devices with their start and end apart: 3, of which 3 were waited for; matrix products, arithmetic and copies ran while one was open for 1% of the time, Pallas kernels for 0%

commit v1 on v0

v1 whole, which is shorter than its diff:
```python
import jax
import jax.numpy as jnp
from jax import lax
from jax.experimental import pallas as pl
from jax.experimental.pallas import tpu as pltpu
from jax.sharding import Mesh, PartitionSpec as P

EPS = 1e-05
F32 = jnp.float32
BF16 = jnp.bfloat16
AXIAL = ("y", "z", "x_hi")
ROWS = 1536
VMEM_LIMIT = 56 * 1024 * 1024

NN = (((1,), (0,)), ((), ()))
NT = (((1,), (1,)), ((), ()))


def mm(a, b, dims=NN):
    return lax.dot_general(a, b, dims, preferred_element_type=F32)


def norm_rows(x):
    average = jnp.mean(x, axis=-1, keepdims=True)
    centered = x - average
    inverse = lax.rsqrt(jnp.mean(centered * centered, axis=-1, keepdims=True) + EPS)
    return centered * inverse, inverse


def project_kernel(
    x_ref, adj_ref, w_ref, wo_ref, gain_ref, shift_ref, gbias_ref,
    qt_ref, kt_ref, vt_ref, k_ref, v_ref, gt_ref, dgt_ref, dat_ref, wt_ref,
):
    @pl.when(pl.program_id(0) == 0)
    def _():
        wt_ref[...] = w_ref[...].astype(F32).T.astype(BF16)

    unit, _ = norm_rows(x_ref[0].astype(F32))
    xn = (unit * gain_ref[...] + shift_ref[...]).astype(BF16)
    factor = 32 ** (-0.5)
    qt_ref[0] = (mm(wt_ref[0:256, :], xn, NT) * factor).astype(BF16)
    kt_ref[0] = mm(wt_ref[256:512, :], xn, NT).astype(BF16)
    vt_ref[0] = mm(wt_ref[512:768, :], xn, NT).astype(BF16)
    k_ref[0] = mm(xn, w_ref[:, 256:512]).astype(BF16)
    v_ref[0] = mm(xn, w_ref[:, 512:768]).astype(BF16)
    gate = jax.nn.sigmoid(mm(wt_ref[768:1024, :], xn, NT) + gbias_ref[...])
    dgated = mm(wo_ref[...], adj_ref[0], NT)
    gt_ref[0] = gate
    dgt_ref[0] = dgated
    dat_ref[0] = (dgated * gate).astype(BF16)


def project(x, adj, w, wo, gain, shift, gbias):
    rows = x.shape[0]
    block = pl.BlockSpec((1, 256, 256), lambda s: (s, 0, 0))
    whole = lambda a: pl.BlockSpec(a.shape, lambda s: (0,) * a.ndim)
    small = jax.ShapeDtypeStruct((rows, 256, 256), BF16)
    big = jax.ShapeDtypeStruct((rows, 256, 256), F32)
    return pl.pallas_call(
        project_kernel,
        grid=(rows,),
        in_specs=[block, block, whole(w), whole(wo), whole(gain), whole(shift), whole(gbias)],
        out_specs=[block] * 8,
        out_shape=[small] * 5 + [big, big, small],
        scratch_shapes=[pltpu.VMEM((1024, 256), BF16)],
        compiler_params=pltpu.CompilerParams(vmem_limit_bytes=VMEM_LIMIT),
        name="project",
    )(x, adj, w, wo, gain, shift, gbias)


def attend_kernel(
    heads, first, rows,
    bias_ref, qt_ref, kt_ref, vt_ref, k_ref, v_ref, gt_ref, dgt_ref, dat_ref,
    dp_ref, gated_ref, dbias_ref, gb_ref, bt_ref, acc_ref, out_ref,
):
    step = pl.program_id(0)

    @pl.when(step == 0)
    def _():
        for h in range(heads):
            for side in range(2):
                part = bias_ref[pl.ds(side * heads + h, 256, stride=2 * heads), :]
                bt_ref[h, 128 * side : 128 * side + 128, :] = part.T
        acc_ref[...] = jnp.zeros_like(acc_ref)
        gb_ref[...] = jnp.zeros_like(gb_ref)

    def own(block, at):
        parts = []
        if at:
            parts.append(jnp.zeros((32 * at, 256), BF16))
        parts.append(block)
        if at < 3:
            parts.append(jnp.zeros((32 * (3 - at), 256), BF16))
        return jnp.concatenate(parts, axis=0)

    for h in range(heads):
        head = first + h
        group, at = head // 4, head % 4
        lanes = slice(128 * group, 128 * group + 128)
        here = slice(32 * head, 32 * head + 32)
        out = slice(32 * h, 32 * h + 32)
        qt = qt_ref[0, here, :]
        kt = kt_ref[0, here, :]
        vt = vt_ref[0, here, :]
        dat = dat_ref[0, here, :]
        st = mm(k_ref[0, :, lanes], own(qt, at)) + bt_ref[h]
        e = jnp.exp(st - jnp.max(st, axis=0, keepdims=True))
        p = e * (1.0 / jnp.sum(e, axis=0, keepdims=True))
        p_low = p.astype(BF16)
        dpt = mm(v_ref[0, :, lanes], own(dat, at))
        delta = jnp.sum(p * dpt, axis=0, keepdims=True)
        ds = p * (dpt - delta)
        acc_ref[h] += ds
        ds_low = ds.astype(BF16)
        att = mm(vt, p_low)
        g = gt_ref[0, here, :]
        graw = dgt_ref[0, here, :] * att * g * (1.0 - g)
        gated_ref[0, out, :] = (g * att).astype(BF16)
        gb_ref[out, :] += graw[:, :128] + graw[:, 128:]
        dp_ref[0, 0, out, :] = (mm(kt, ds_low) * (32 ** (-0.5))).astype(BF16)
        dp_ref[0, 1, out, :] = mm(qt, ds_low, NT).astype(BF16)
        dp_ref[0, 2, out, :] = mm(dat, p_low, NT).astype(BF16)
        dp_ref[0, 3, out, :] = graw.astype(BF16)

    @pl.when(step == rows - 1)
    def _():
        for h in range(heads):
            for side in range(2):
                part = acc_ref[h, 128 * side : 128 * side + 128, :]
                out_ref[pl.ds(side * heads + h, 256, stride=2 * heads), :] = part.T
        dbias_ref[...] = out_ref[...].astype(BF16)


def attend(bias, qt, kt, vt, k, v, gt, dgt, dat, first, heads):
    rows = qt.shape[0]
    block = pl.BlockSpec((1, 256, 256), lambda s: (s, 0, 0))
    width = 32 * heads

    def kernel(*refs):
        attend_kernel(heads, first, rows, *refs)

    return pl.pallas_call(
        kernel,
        grid=(rows,),
        in_specs=[pl.BlockSpec((512 * heads, 128), lambda s: (0, 0))] + [block] * 8,
        out_specs=[
            pl.BlockSpec((1, 4, width, 256), lambda s: (s, 0, 0, 0)),
            pl.BlockSpec((1, width, 256), lambda s: (s, 0, 0)),
            pl.BlockSpec((512 * heads, 128), lambda s: (0, 0)),
            pl.BlockSpec((width, 128), lambda s: (0, 0)),
        ],
        out_shape=[
            jax.ShapeDtypeStruct((rows, 4, width, 256), BF16),
            jax.ShapeDtypeStruct((rows, width, 256), BF16),
            jax.ShapeDtypeStruct((512 * heads, 128), BF16),
            jax.ShapeDtypeStruct((width, 128), F32),
        ],
        scratch_shapes=[
            pltpu.VMEM((heads, 256, 256), F32),
            pltpu.VMEM((heads, 256, 256), F32),
            pltpu.VMEM((512 * heads, 128), F32),
        ],
        compiler_params=pltpu.CompilerParams(vmem_limit_bytes=VMEM_LIMIT),
        name="attend",
    )(bias, qt, kt, vt, k, v, gt, dgt, dat)


def finish_kernel(
    rows, x_ref, adj_ref, w_ref, gain_ref, shift_ref, gb_ref, dp_ref, gated_ref,
    dx_ref, grad_ref, acc_ref, wo_ref, mg_ref, mb_ref,
):
    step = pl.program_id(0)

    @pl.when(step == 0)
    def _():
        acc_ref[...] = jnp.zeros_like(acc_ref)
        wo_ref[...] = jnp.zeros_like(wo_ref)
        mg_ref[...] = jnp.zeros_like(mg_ref)
        mb_ref[...] = jnp.zeros_like(mb_ref)

    unit, inverse = norm_rows(x_ref[0].astype(F32))
    gain = gain_ref[...]
    xn = (unit * gain + shift_ref[...]).astype(BF16)
    dp = dp_ref[0]
    acc_ref[...] += mm(dp, xn)
    wo_ref[...] += mm(gated_ref[0], adj_ref[0])
    dn = mm(w_ref[...], dp).T
    mg_ref[...] += jnp.sum(unit * dn, axis=0, keepdims=True)
    mb_ref[...] += jnp.sum(dn, axis=0, keepdims=True)
    g = dn * gain
    mean = jnp.mean(g, axis=-1, keepdims=True)
    cross = jnp.mean(g * unit, axis=-1, keepdims=True)
    dx_ref[0] = (inverse * (g - mean - unit * cross)).astype(BF16)

    @pl.when(step == rows - 1)
    def _():
        gb = jnp.sum(gb_ref[...].T, axis=0, keepdims=True)
        vectors = jnp.concatenate([gb, mg_ref[...], mb_ref[...], jnp.zeros((5, 256), F32)], axis=0)
        for side in range(2):
            lanes = slice(128 * side, 128 * side + 128)
            grad_ref[side, 0:1024, :] = acc_ref[:, lanes]
            grad_ref[side, 1024:1280, :] = wo_ref[:, lanes]
            grad_ref[side, 1280:1288, :] = vectors[:, lanes]
            grad_ref[side, 1288:ROWS, :] = jnp.zeros((ROWS - 1288, 128), F32)


def finish(x, adj, w, gain, shift, gb, dp, gated):
    rows = x.shape[0]
    block = pl.BlockSpec((1, 256, 256), lambda s: (s, 0, 0))
    whole = lambda a: pl.BlockSpec(a.shape, lambda s: (0,) * a.ndim)

    def kernel(*refs):
        finish_kernel(rows, *refs)

    return pl.pallas_call(
        kernel,
        grid=(rows,),
        in_specs=[
            block, block, whole(w), whole(gain), whole(shift), whole(gb),
            pl.BlockSpec((1, 1024, 256), lambda s: (s, 0, 0)), block,
        ],
        out_specs=[block, pl.BlockSpec((2, ROWS, 128), lambda s: (0, 0, 0))],
        out_shape=[
            jax.ShapeDtypeStruct((rows, 256, 256), BF16),
            jax.ShapeDtypeStruct((2, ROWS, 128), F32),
        ],
        scratch_shapes=[
            pltpu.VMEM((1024, 256), F32),
            pltpu.VMEM((256, 256), F32),
            pltpu.VMEM((1, 256), F32),
            pltpu.VMEM((1, 256), F32),
        ],
        compiler_params=pltpu.CompilerParams(vmem_limit_bytes=VMEM_LIMIT),
        name="finish",
    )(x, adj, w, gain, shift, gb, dp, gated)


def local(x, pair, adj, w, gbias, wo, gain, shift, pair_gain, pair_w):
    x, adj, pair = x[0], adj[0], pair[0]
    unit, inverse = norm_rows(pair.astype(F32))
    pn = (unit * pair_gain).astype(BF16)
    own = jnp.einsum("ijc,ch->ihj", pn, pair_w, preferred_element_type=F32)
    own = own.reshape(4, 8, 2, 128).transpose(0, 2, 1, 3).reshape(64, 128)
    bias = own
    for axis in ("x_hi", "z", "y"):
        bias = lax.all_gather(bias, axis, tiled=True)

    gain2, shift2 = gain.reshape(1, 256), shift.reshape(1, 256)
    qt, kt, vt, k, v, gt, dgt, dat = project(x, adj, w, wo, gain2, shift2, gbias.reshape(256, 1))
    dp, gated, dbias, gb = attend(bias, qt, kt, vt, k, v, gt, dgt, dat, 0, 8)
    dx, grad = finish(x, adj, w, gain2, shift2, gb, dp.reshape(8, 1024, 256), gated)

    blocks = lax.all_to_all(dbias, AXIAL, 0, 0, tiled=True)
    d_local = jnp.sum(blocks.reshape(64, 64, 128).astype(F32), axis=0)
    d_local = d_local.reshape(4, 2, 8, 128).transpose(0, 2, 1, 3).reshape(4, 8, 256)
    dpn = jnp.einsum("ihj,ch->ijc", d_local, pair_w.astype(F32))
    d_wb = jnp.einsum("ijc,ihj->hc", pn.astype(F32), d_local)
    d_pg = jnp.sum(unit * dpn, axis=(0, 1))
    g = dpn * pair_gain
    mean = jnp.mean(g, axis=-1, keepdims=True)
    cross = jnp.mean(g * unit, axis=-1, keepdims=True)
    dpair = (inverse * (g - mean - unit * cross)).astype(BF16)

    extra = jnp.concatenate([d_wb, d_pg[None], jnp.zeros((7, 128), F32)], axis=0)
    grad = lax.dynamic_update_slice(grad, extra[None], (0, 1288, 0))
    half = jnp.sum(lax.all_to_all(grad, "core", 0, 0, tiled=True), axis=0)
    parts = lax.all_to_all(half.astype(BF16), AXIAL, 0, 0, tiled=True)
    mine = jnp.sum(parts.reshape(64, ROWS // 64, 128).astype(F32), axis=0)
    mine = mine + lax.ppermute(mine, "x_lo", [(0, 1), (1, 0)])
    total = mine
    for axis in ("x_hi", "z", "y"):
        total = lax.all_gather(total, axis, tiled=True)
    total = lax.all_gather(total, "core")
    f = float(524288) ** (-0.5)
    fp = float(262144) ** (-0.5)
    joined = jnp.concatenate([total[0, :1288], total[1, :1288]], axis=1) * f
    return (
        dx[None],
        dpair[None],
        joined[:1024].T,
        joined[1280],
        joined[1024:1280],
        joined[1281],
        joined[1282],
        total[0, 1296] * fp,
        total[0, 1288:1296].T * fp,
    )


def solution(mesh):
    fine = Mesh(mesh.devices.reshape(2, 2, 4, 8, 2), ("x_lo", "core", "y", "z", "x_hi"))
    split = P(("x_lo", "core"), AXIAL)
    return jax.shard_map(
        local,
        mesh=fine,
        in_specs=(split,) * 3 + (P(),) * 7,
        out_specs=(split, split) + (P(),) * 7,
        check_vma=False,
    )
```

time: 1100 us -> 259 us (0.24)
  waiting for transfers between devices: 739 us -> 54.3 us
  matrix products: 140 us -> 2.24 us
  other arithmetic: 73.8 us -> 3.29 us
  Pallas kernels: 0 us -> 53.3 us
  local copies, waits for them, and re-layouts: 58 us -> 6.87 us
  blocking collectives: 71.5 us -> 110 us
  starting transfers between devices: 0.12 us -> 12.3 us
    reduce_scatter x1 -> x0, waiting for transfers between devices: 363 us -> none  [local(): lax.psum_scatter(bias_gradient[None], 'axial', scatter_dimension=2, tiled...]
    psum x1 -> x0, waiting for transfers between devices: 254 us -> none  [local(): lax.psum((gradient_tree[0], gradient_tree[1], gradient_tree[2], gradient_...]
    dot_general x91 -> x3, matrix products: 140 us -> 2.24 us  [the longest x1 1.13 us: local(): dpn = jnp.einsum('ihj,ch->ijc', d_local, pair_w.astype(F32))]
    all_gather x1 -> x2, waiting for transfers between devices: 122 us -> 31.8 us  [the longest x1 22.2 us: local(): bias = lax.all_gather(bias, axis, tiled=True)]
    all_gather x0 -> x5, blocking collectives: none -> 82 us  [the longest x3 44.8 us: local(): total = lax.all_gather(total, axis, tiled=True)]
    psum x1 -> x0, blocking collectives: 71.5 us -> none  [local(): lax.psum((gradient_tree[0], gradient_tree[1], gradient_tree[2], gradient_...]
    pallas_call x0 -> x3, Pallas kernels: none -> 53.3 us  [the longest x1 33.4 us: attend(): pl.pallas_call(kernel, grid=(rows,), in_specs=[pl.BlockSpec((512 * heads,...]
    all_to_all x0 -> x2, blocking collectives: none -> 27.7 us  [the longest x1 22.7 us: local(): parts = lax.all_to_all(half.astype(BF16), AXIAL, 0, 0, tiled=True)]
  transfers between devices with their start and end apart: 3 -> 4, of which waited for: 3 -> 4; matrix products, arithmetic and copies ran while one was open for 1% -> 1% of each run, Pallas kernels for 0% -> 8%
where the time goes in v1:
time: 259 us; the launch traced here: 256 us
  blocking collectives  110 us (42%)
  waiting for transfers between devices  54.3 us (21%)
  Pallas kernels  53.3 us (21%)
  between operations  14.2 us (5%)
  starting transfers between devices  12.3 us (5%)
  local copies, waits for them, and re-layouts  6.87 us (3%)
  other arithmetic  3.29 us (1%)
    all_gather x3, blocking collectives, local(): total = lax.all_gather(total, axis, tiled=True)  44.8 us
    all_gather x2, blocking collectives, local(): bias = lax.all_gather(bias, axis, tiled=True)  37.2 us
    pallas_call x1, Pallas kernels, attend(): pl.pallas_call(kernel, grid=(rows,), in_specs=[pl.BlockSpec((512 * heads,...  33.4 us
    all_to_all x1, blocking collectives, local(): parts = lax.all_to_all(half.astype(BF16), AXIAL, 0, 0, tiled=True)  22.7 us
    all_gather x1, waiting for transfers between devices, local(): bias = lax.all_gather(bias, axis, tiled=True)  22.2 us
    all_to_all x1, waiting for transfers between devices, local(): blocks = lax.all_to_all(dbias, AXIAL, 0, 0, tiled=True)  20.2 us
    all_to_all x1, starting transfers between devices, local(): blocks = lax.all_to_all(dbias, AXIAL, 0, 0, tiled=True)  10.7 us
    pallas_call x1, Pallas kernels, finish(): pl.pallas_call(kernel, grid=(rows,), in_specs=[block, block, whole(w), wh...  10.1 us
  transfers between devices with their start and end apart: 4, of which 4 were waited for; matrix products, arithmetic and copies ran while one was open for 1% of the time, Pallas kernels for 8%

profile of v1, /device:TPU:2, one launch (start us, length us, event | category | flops | bytes accessed | tf_op | source)
XLA Modules:
  0.0 256.2 jit_solution(5479406393748857338)
XLA Ops:
  7.2 0.0 copy-start
  7.2 0.0 copy-start.3
  7.2 0.0 all-gather.4.cloned.1.call-start
  7.2 1.1 copy.30
  8.3 0.1 convert_reduce_fusion.2
  8.4 0.1 fusion.13
  8.5 0.0 copy-done
  8.5 0.9 fusion.23
  9.4 6.1 %all_gather.24 = f32[128,128]{1,0:T(8,128)S(1)} all-gather(f32[64,128]{1,0:T(8,128)S(1)} %bitcast.101), channel_id=1, replica_groups=mesh['x_lo'=2,'core'=2,'y'=4,'z'=8,'x_hi'=2] {'x_hi'}, dimensions={0}, use_global_device_ids=true | all-gather | bytes 98304 | tf_op jit(solution)/shard_map/all_gather | solution.py:246
  15.5 31.2 %all_gather.25 = f32[1024,128]{1,0:T(8,128)} all-gather(f32[128,128]{1,0:T(8,128)S(1)} %all_gather.24), channel_id=1, replica_groups=mesh['x_lo'=2,'core'=2,'y'=4,'z'=8,'x_hi'=2] {'z'}, dimensions={0}, use_global_device_ids=true | all-gather | bytes 589824 | tf_op jit(solution)/shard_map/all_gather | solution.py:246
  46.6 0.0 all-gather.4.cloned.1.call-update
  46.7 0.0 copy-done.3
  46.7 0.8 copy.32.gbias_ref
  47.5 9.8 %project.1 = (bf16[8,256,256]{2,1,0:T(8,128)(2,1)}, bf16[8,256,256]{2,1,0:T(8,128)(2,1)}, bf16[8,256,256]{2,1,0:T(8,128)(2,1)}, bf16[8,256,256]{2,1,0:T(8,128)(2...) custom-call(bf16[8,256,256]{2,1,0:T(8,128)(2,1)} %bitcast.91, ...), custom_call_target="tpu_custom_call" | custom-call | tf_op jit(solution)/shard_map/project/pallas_call | solution.py:59
  57.3 22.2 %all-gather.4.cloned.1.call-done.refs_0_ = f32[4096,128]{1,0:T(8,128)} async-done(((f32[1024,128]{1,0:T(8,128)}), f32[4096,128]{1,0:T(8,128)}) %all-gather.4.cloned.1.call-update) | async-done | bytes 2097168 | tf_op jit(solution)/shard_map/all_gather | solution.py:246
  79.5 33.4 %attend.1 = (bf16[8,4,256,256]{3,2,1,0:T(8,128)(2,1)}, bf16[8,256,256]{2,1,0:T(8,128)(2,1)}, bf16[4096,128]{1,0:T(8,128)(2,1)}, f32[256,128]{1,0:T(8,128)}) custom-call(f32[4096,128]{1,0:T(8,128)} %all-gather.4.cloned.1.call-done.refs_0_, bf16[8,256,256]{2,1,0:T(8,128)(2,1)} %get-tuple-element.23.refs_1_, bf16[8,256,256]{2,1,0:T(8,128)(2,1)} %get-tuple-element.24.refs_2_, ...), custom_call_target="tpu_custom_call" | custom-call | tf_op jit(solution)/shard_map/attend/pallas_call | solution.py:142
  112.9 10.7 %all-to-all-start = ((bf16[64,64,128]{2,1,0:T(8,128)(2,1)}), bf16[64,64,128]{2,1,0:T(8,128)(2,1)S(1)}, u32[]{:S(2)}, u32[]{:S(2)}) async-start(bf16[64,64,128]{2,1,0:T(8,128)(2,1)} %bitcast.100), calls=%async_computation | async-start | bytes 2097152 | tf_op jit(solution)/shard_map/all_to_all | solution.py:253
  123.6 0.0 all-gather.6.cloned.1.call-start
  123.7 0.1 pad.4.clone
  123.7 0.0 copy-start.4
  123.8 10.1 %finish.1 = (bf16[8,256,256]{2,1,0:T(8,128)(2,1)}, f32[2,1536,128]{2,1,0:T(8,128)}) custom-call(bf16[8,256,256]{2,1,0:T(8,128)(2,1)} %bitcast.92, bf16[8,256,256]{2,1,0:T(8,128)(2,1)} %bitcast.94, bf16[256,1024]{1,0:T(8,128)(2,1)} %refs_2_.1, f32[1,256]{1,0:T(1,128)} %bitcast.105, f32[1,256]{1,0:T(1,128)} %bitcast.107, ...), custom_call_target="tpu_custom_call" | custom-call | tf_op jit(solution)/shard_map/finish/pallas_call | solution.py:215
  133.9 0.0 copy-start.1
  133.9 20.2 %all-to-all-done = bf16[64,64,128]{2,1,0:T(8,128)(2,1)S(1)} async-done(((bf16[64,64,128]{2,1,0:T(8,128)(2,1)}), bf16[64,64,128]{2,1,0:T(8,128)(2,1)S(1)}, u32[]{:S(2)}, u32[]{:S(2)}) %all-to-all-start) | async-done | bytes 1048608 | tf_op jit(solution)/shard_map/all_to_all | solution.py:253
  154.1 0.2 convert_reduce_fusion
  154.2 0.0 copy-done.4
  154.3 1.1 fusion.12
  155.4 0.2 convolution_bitcast_fusion
  155.6 0.0 copy-done.1
  155.6 0.1 fusion.25
  155.7 5.0 %all_to_all.20 = f32[2,1536,128]{2,1,0:T(8,128)S(1)} all-to-all(f32[2,1536,128]{2,1,0:T(8,128)S(1)} %fusion.25), channel_id=1, replica_groups=mesh['x_lo'=2,'core'=2,'y'=4,'z'=8,'x_hi'=2] {'core'}, dimensions={0} | all-to-all | bytes 3145728 | tf_op jit(solution)/shard_map/all_to_all | solution.py:266
  160.7 0.1 reduce_sum.78
  160.8 0.0 copy-start.2
  160.8 22.7 %all_to_all.21 = bf16[64,24,128]{2,1,0:T(8,128)(2,1)S(1)} all-to-all(bf16[64,24,128]{2,1,0:T(8,128)(2,1)S(1)} %bitcast.96), channel_id=1, replica_groups=mesh['x_lo'=2,'core'=2,'y'=4,'z'=8,'x_hi'=2] {'y','z','x_hi'}, dimensions={0} | all-to-all | bytes 786432 | tf_op jit(solution)/shard_map/all_to_all | solution.py:267
  183.4 0.1 convert_reduce_fusion.1
  183.5 1.5 collective-permute-start
  185.1 2.2 collective-permute-done
  187.3 5.9 %all_gather.27 = f32[48,128]{1,0:T(8,128)S(1)} all-gather(f32[24,128]{1,0:T(8,128)S(1)} %add.16), channel_id=1, replica_groups=mesh['x_lo'=2,'core'=2,'y'=4,'z'=8,'x_hi'=2] {'x_hi'}, dimensions={0}, use_global_device_ids=true | all-gather | bytes 36864 | tf_op jit(solution)/shard_map/all_gather | solution.py:272
  193.2 24.9 %all_gather.28 = f32[384,128]{1,0:T(8,128)S(1)} all-gather(f32[48,128]{1,0:T(8,128)S(1)} %all_gather.27), channel_id=1, replica_groups=mesh['x_lo'=2,'core'=2,'y'=4,'z'=8,'x_hi'=2] {'z'}, dimensions={0}, use_global_device_ids=true | all-gather | bytes 221184 | tf_op jit(solution)/shard_map/all_gather | solution.py:272
  218.1 14.0 %all_gather.29 = f32[1536,128]{1,0:T(8,128)} all-gather(f32[384,128]{1,0:T(8,128)S(1)} %all_gather.28), channel_id=1, replica_groups=mesh['x_lo'=2,'core'=2,'y'=4,'z'=8,'x_hi'=2] {'y'}, dimensions={0}, use_global_device_ids=true | all-gather | bytes 983040 | tf_op jit(solution)/shard_map/all_gather | solution.py:272
  232.1 0.0 all-gather.6.cloned.1.call-update
  232.1 0.0 copy-done.2
  232.1 0.2 fusion.19
  232.3 0.8 copy.34
  233.2 9.6 %all-gather.6.cloned.1.call-done = f32[3072,128]{1,0:T(8,128)} async-done(((f32[1536,128]{1,0:T(8,128)}), f32[3072,128]{1,0:T(8,128)}) %all-gather.6.cloned.1.call-update) | async-done | bytes 1572880 | tf_op jit(solution)/shard_map/all_gather | solution.py:273
  242.7 1.4 slice_bitcast_fusion.2
  244.1 0.1 maximum_multiply_fusion
  244.2 0.1 slice_bitcast_fusion
  244.3 0.7 slice.40
  245.0 0.6 fusion.31
  245.6 1.3 fusion.26
  246.9 1.2 fusion.30
  248.0 1.3 copy.35
  (5 shorter events, 0.0 us)
Async XLA Ops:
  7.2 1.3 copy-start
  7.2 39.5 %copy-start.3 = (f32[256]{0:T(256)S(1)}, f32[256]{0:T(256)}, u32[]{:S(2)}) copy-start(f32[256]{0:T(256)} %param.14) | copy-start | bytes 3076
  7.2 72.3 %all-gather.4.cloned.1.call-start = ((), (), s32[]{:S(2)}) async-start(), calls=%async_computation.3 | async-start | bytes 2621440 | tf_op jit(solution)/shard_map/all_gather | solution.py:246
  112.9 41.2 %all-to-all-start = ((bf16[64,64,128]{2,1,0:T(8,128)(2,1)}), bf16[64,64,128]{2,1,0:T(8,128)(2,1)S(1)}, u32[]{:S(2)}, u32[]{:S(2)}) async-start(bf16[64,64,128]{2,1,0:T(8,128)(2,1)} %bitcast.100), calls=%async_computation | async-start | bytes 2097152 | tf_op jit(solution)/shard_map/all_to_all | solution.py:253
  123.6 119.1 %all-gather.6.cloned.1.call-start = ((), (), s32[]{:S(2)}) async-start(), calls=%async_computation.4 | async-start | bytes 2359296 | tf_op jit(solution)/shard_map/all_gather | solution.py:273
  123.7 30.5 %copy-start.4 = (f32[128]{0:T(128)S(1)}, f32[128]{0:T(128)}, u32[]{:S(2)}) copy-start(f32[128]{0:T(128)} %param.18) | copy-start | bytes 1540
  133.9 21.8 %copy-start.1 = (f32[2,1536,128]{2,1,0:T(8,128)S(1)}, f32[2,1536,128]{2,1,0:T(8,128)}, u32[]{:S(2)}) copy-start(f32[2,1536,128]{2,1,0:T(8,128)} %get-tuple-element.36) | copy-start | bytes 4718596
  160.8 71.4 %copy-start.2 = (f32[4,256,128]{1,2,0:T(8,128)S(1)}, f32[4,256,128]{1,2,0:T(8,128)}, u32[]{:S(2)}) copy-start(f32[4,256,128]{1,2,0:T(8,128)} %get-tuple-element.72) | copy-start | bytes 1572868
  183.5 3.8 %collective-permute-start = (f32[24,128]{1,0:T(8,128)S(1)}, f32[24,128]{1,0:T(8,128)S(1)}, u32[]{:S(2)}, u32[]{:S(2)}) collective-permute-start(f32[24,128]{1,0:T(8,128)S(1)} %convert_reduce_fusion.1), channel_id=1, source_target_pairs={{0,128},{128,0},{1,129},{129,1},{2,130},{130,2},{3,131},{131,3},{4... | collective-permute-start | bytes 36872 | tf_op jit(solution)/shard_map/ppermute | solution.py:269
Sparse Core Ops, SparseCore 0:
  46.8 32.6 all-gather.3
  232.2 10.4 all-gather.5

commit v2 on v1

v2 whole, which is shorter than its diff:
```python
import jax
import jax.numpy as jnp
from jax import lax
from jax.experimental import pallas as pl
from jax.experimental.pallas import tpu as pltpu
from jax.sharding import Mesh, PartitionSpec as P

EPS = 1e-05
F32 = jnp.float32
BF16 = jnp.bfloat16
AXIAL = ("y", "z", "x_hi")
PLANE = ("y", "x_hi")
SENT = [(y * 2 + x) * 8 + z for y in range(4) for z in range(8) for x in range(2)]
TINY = pl.CostEstimate(flops=1000, bytes_accessed=1000, transcendentals=0)
VMEM_LIMIT = 56 * 1024 * 1024

NN = (((1,), (0,)), ((), ()))
NT = (((1,), (1,)), ((), ()))


def mm(a, b, dims=NN):
    return lax.dot_general(a, b, dims, preferred_element_type=F32)


def norm_rows(x):
    average = jnp.mean(x, axis=-1, keepdims=True)
    centered = x - average
    inverse = lax.rsqrt(jnp.mean(centered * centered, axis=-1, keepdims=True) + EPS)
    return centered * inverse, inverse


def project_kernel(
    x_ref, adj_ref, w_ref, wo_ref, gain_ref, shift_ref, gbias_ref, column_ref,
    qt_ref, kt_ref, vt_ref, k_ref, v_ref, gt_ref, dgt_ref, dat_ref, xn_ref, copies_ref, wt_ref, gcol_ref,
):
    @pl.when(pl.program_id(0) == 0)
    def _():
        wt_ref[...] = w_ref[...].astype(F32).T.astype(BF16)
        gcol_ref[...] = jnp.broadcast_to(gbias_ref[...], (128, 256)).T
        for r in range(8):
            for z in range(8):
                copies_ref[r, 32 * z : 32 * z + 32, :] = column_ref[z, 32:64, :]

    unit, _ = norm_rows(x_ref[0].astype(F32))
    xn = (unit * gain_ref[...] + shift_ref[...]).astype(BF16)
    xn_ref[0] = xn
    factor = 32 ** (-0.5)
    qt_ref[0] = (mm(wt_ref[0:256, :], xn, NT) * factor).astype(BF16)
    kt_ref[0] = mm(wt_ref[256:512, :], xn, NT).astype(BF16)
    vt_ref[0] = mm(wt_ref[512:768, :], xn, NT).astype(BF16)
    k_ref[0] = mm(xn, w_ref[:, 256:512]).astype(BF16)
    v_ref[0] = mm(xn, w_ref[:, 512:768]).astype(BF16)
    shifted = jnp.concatenate([gcol_ref[...], gcol_ref[...]], axis=1)
    gate = jax.nn.sigmoid(mm(wt_ref[768:1024, :], xn, NT) + shifted)
    dgated = mm(wo_ref[...], adj_ref[0], NT)
    gt_ref[0] = gate
    dgt_ref[0] = dgated
    dat_ref[0] = (dgated * gate).astype(BF16)


def project(x, adj, w, wo, gain, shift, gbias, column):
    rows = x.shape[0]
    block = pl.BlockSpec((1, 256, 256), lambda s: (s, 0, 0))
    whole = lambda a: pl.BlockSpec(a.shape, lambda s: (0,) * a.ndim)
    small = jax.ShapeDtypeStruct((rows, 256, 256), BF16)
    big = jax.ShapeDtypeStruct((rows, 256, 256), F32)
    return pl.pallas_call(
        project_kernel,
        grid=(rows,),
        in_specs=[block, block, whole(w), whole(wo), whole(gain), whole(shift), whole(gbias), whole(column)],
        out_specs=[block] * 9 + [pl.BlockSpec((8, 256, 128), lambda s: (0, 0, 0))],
        out_shape=[small] * 5 + [big, big, small, small, jax.ShapeDtypeStruct((8, 256, 128), F32)],
        scratch_shapes=[pltpu.VMEM((1024, 256), BF16), pltpu.VMEM((256, 128), F32)],
        compiler_params=pltpu.CompilerParams(vmem_limit_bytes=VMEM_LIMIT),
        cost_estimate=TINY,
        name="project",
    )(x, adj, w, wo, gain, shift, gbias, column)


def attend_kernel(
    heads, first, rows, last,
    bias_ref, qt_ref, kt_ref, vt_ref, k_ref, v_ref, gt_ref, dgt_ref, dat_ref, xn_ref, adj_ref, *refs
):
    if last:
        other_ref, dp_ref, gb_ref, send_ref, bt_ref, acc_ref, out_ref, w_ref, stage_ref = refs
    else:
        dp_ref, gb_ref, send_ref, grad_ref, bt_ref, acc_ref, out_ref, w_ref = refs
    step = pl.program_id(0)
    width = 32 * heads

    @pl.when(step == 0)
    def _():
        for natural, sent in enumerate(SENT):
            out_ref[32 * natural : 32 * natural + 32, :] = bias_ref[32 * sent : 32 * sent + 32, :]
        for h in range(heads):
            for side in range(2):
                part = out_ref[pl.ds(side * heads + h, 256, stride=2 * heads), :]
                bt_ref[h, 128 * side : 128 * side + 128, :] = part.T
        acc_ref[...] = jnp.zeros_like(acc_ref)
        gb_ref[...] = jnp.zeros_like(gb_ref)
        w_ref[...] = jnp.zeros_like(w_ref)

    def own(block, at):
        parts = []
        if at:
            parts.append(jnp.zeros((32 * at, 256), BF16))
        parts.append(block)
        if at < 3:
            parts.append(jnp.zeros((32 * (3 - at), 256), BF16))
        return jnp.concatenate(parts, axis=0)

    gated = [[] for _ in range(2)]

    def place(h):
        head = first + h
        return slice(32 * head, 32 * head + 32), head // 4, head % 4

    def score(r, h):
        here, group, at = place(h)
        lanes = slice(128 * group, 128 * group + 128)
        st = mm(k_ref[r, :, lanes], own(qt_ref[r, here, :], at))
        dpt = mm(v_ref[r, :, lanes], own(dat_ref[r, here, :], at))
        return st, dpt

    def soft(r, h, st, dpt):
        st = st + bt_ref[h]
        e = jnp.exp(st - jnp.max(st, axis=0, keepdims=True))
        p = e * (1.0 / jnp.sum(e, axis=0, keepdims=True))
        delta = jnp.sum(p * dpt, axis=0, keepdims=True)
        ds = p * (dpt - delta)
        acc_ref[h] += ds
        return p.astype(BF16), ds.astype(BF16)

    def half_soft(r, h, st, dpt):
        ps, dss = [], []
        for side in range(2):
            at = slice(128 * side, 128 * side + 128)
            x = st[:, at] + bt_ref[h, :, at]
            e = jnp.exp(x - jnp.max(x, axis=0, keepdims=True))
            p = e * (1.0 / jnp.sum(e, axis=0, keepdims=True))
            d = dpt[:, at]
            delta = jnp.sum(p * d, axis=0, keepdims=True)
            ds = p * (d - delta)
            acc_ref[h, :, at] += ds
            ps.append(p.astype(BF16))
            dss.append(ds.astype(BF16))
        return jnp.concatenate(ps, axis=1), jnp.concatenate(dss, axis=1)

    def close(r, h, p_low, ds_low):
        here, _, _ = place(h)
        out = slice(32 * h, 32 * h + 32)
        att = mm(vt_ref[r, here, :], p_low)
        g = gt_ref[r, here, :]
        graw = dgt_ref[r, here, :] * att * g * (1.0 - g)
        gated[r].append((g * att).astype(BF16))
        gb_ref[out, :] += graw[:, :128] + graw[:, 128:]
        dp_ref[r, 0, out, :] = (mm(kt_ref[r, here, :], ds_low) * (32 ** (-0.5))).astype(BF16)
        dp_ref[r, 1, out, :] = mm(qt_ref[r, here, :], ds_low, NT).astype(BF16)
        dp_ref[r, 2, out, :] = mm(dat_ref[r, here, :], p_low, NT).astype(BF16)
        dp_ref[r, 3, out, :] = graw.astype(BF16)

    items = [(r, h) for r in range(2) for h in range(heads)]
    scores = [score(*items[0])]
    lows = []
    for n, item in enumerate(items):
        if n + 1 < len(items):
            scores.append(score(*items[n + 1]))
        lows.append(half_soft(*item, *scores[n]))
        if n:
            close(*items[n - 1], *lows[n - 1])
    close(*items[-1], *lows[-1])

    xn = xn_ref[...].reshape(256 * 2, 256)
    for b in range(4):
        both = jnp.concatenate([dp_ref[r, b] for r in range(2)], axis=1)
        w_ref[width * b : width * b + width, :] += mm(both, xn)
    both = jnp.concatenate([jnp.concatenate(g, axis=0) for g in gated], axis=1)
    w_ref[4 * width : 5 * width, :] += mm(both, adj_ref[...].reshape(256 * 2, 256))

    @pl.when(step == rows // 2 - 1)
    def _():
        for h in range(heads):
            for side in range(2):
                part = acc_ref[h, 128 * side : 128 * side + 128, :]
                out_ref[pl.ds(side * heads + h, 256, stride=2 * heads), :] = part.T
        if not last:
            for natural, sent in enumerate(SENT):
                send_ref[sent] = out_ref[32 * natural : 32 * natural + 32, :].astype(BF16)
            for side in range(2):
                grad_ref[side] = w_ref[:, 128 * side : 128 * side + 128]
        else:
            for natural, sent in enumerate(SENT):
                stage_ref[sent, 0:32, :] = out_ref[32 * natural : 32 * natural + 32, :]
            for side in range(2):
                for b in range(5):
                    for c in range(2):
                        for r in range(16):
                            g8 = 160 * side + 32 * b + 16 * c + r
                            at = 128 * b + 8 * r
                            if c:
                                piece = w_ref[at : at + 8, 128 * side : 128 * side + 128]
                            else:
                                piece = other_ref[side, at : at + 8, :]
                            to = 32 + 8 * (g8 % 5)
                            stage_ref[g8 // 5, to : to + 8, :] = piece
            send_ref[...] = stage_ref[...].astype(BF16)


def attend(bias, qt, kt, vt, k, v, gt, dgt, dat, xn, adj, first, other):
    rows, heads = qt.shape[0], 4
    last = other is not None
    block = pl.BlockSpec((2, 256, 256), lambda s: (s, 0, 0))
    width = 32 * heads

    def kernel(*refs):
        attend_kernel(heads, first, rows, last, *refs)

    in_specs = [pl.BlockSpec((512 * heads, 128), lambda s: (0, 0))] + [block] * 10
    out_specs = [
        pl.BlockSpec((2, 4, width, 256), lambda s: (s, 0, 0, 0)),
        pl.BlockSpec((width, 128), lambda s: (0, 0)),
    ]
    out_shape = [
        jax.ShapeDtypeStruct((rows, 4, width, 256), BF16),
        jax.ShapeDtypeStruct((width, 128), F32),
    ]
    scratch = [
        pltpu.VMEM((heads, 256, 256), F32),
        pltpu.VMEM((heads, 256, 256), F32),
        pltpu.VMEM((512 * heads, 128), F32),
        pltpu.VMEM((5 * width, 256), F32),
    ]
    operands = [bias, qt, kt, vt, k, v, gt, dgt, dat, xn, adj]
    if last:
        in_specs.append(pl.BlockSpec((2, 5 * width, 128), lambda s: (0, 0, 0)))
        out_specs.append(pl.BlockSpec((64, 72, 128), lambda s: (0, 0, 0)))
        out_shape.append(jax.ShapeDtypeStruct((64, 72, 128), BF16))
        scratch.append(pltpu.VMEM((64, 72, 128), F32))
        operands.append(other)
    else:
        out_specs.append(pl.BlockSpec((64, 8 * heads, 128), lambda s: (0, 0, 0)))
        out_shape.append(jax.ShapeDtypeStruct((64, 8 * heads, 128), BF16))
        out_specs.append(pl.BlockSpec((2, 5 * width, 128), lambda s: (0, 0, 0)))
        out_shape.append(jax.ShapeDtypeStruct((2, 5 * width, 128), F32))
    return pl.pallas_call(
        kernel,
        grid=(rows // 2,),
        in_specs=in_specs,
        out_specs=out_specs,
        out_shape=out_shape,
        scratch_shapes=scratch,
        compiler_params=pltpu.CompilerParams(vmem_limit_bytes=VMEM_LIMIT),
        cost_estimate=TINY,
        name="attend",
    )(*operands)


def inputs_kernel(
    rows, x_ref, w_ref, gain_ref, dpa_ref, dpb_ref, gba_ref, gbb_ref,
    dx_ref, small_ref, mg_ref, mb_ref,
):
    step = pl.program_id(0)

    @pl.when(step == 0)
    def _():
        mg_ref[...] = jnp.zeros_like(mg_ref)
        mb_ref[...] = jnp.zeros_like(mb_ref)

    unit, inverse = norm_rows(x_ref[0].astype(F32))
    gain = gain_ref[...]
    dp = jnp.concatenate([r[0, b] for b in range(4) for r in (dpa_ref, dpb_ref)], axis=0)
    dn = mm(w_ref[...], dp).T
    mg_ref[...] += jnp.sum(unit * dn, axis=0, keepdims=True)
    mb_ref[...] += jnp.sum(dn, axis=0, keepdims=True)
    g = dn * gain
    mean = jnp.mean(g, axis=-1, keepdims=True)
    cross = jnp.mean(g * unit, axis=-1, keepdims=True)
    dx_ref[0] = (inverse * (g - mean - unit * cross)).astype(BF16)

    @pl.when(step == rows - 1)
    def _():
        gb = [jnp.sum(r[...].T, axis=0, keepdims=True) for r in (gba_ref, gbb_ref)]
        mg, mb = mg_ref[...], mb_ref[...]
        small_ref[...] = jnp.concatenate(
            gb + [mg[:, :128], mg[:, 128:], mb[:, :128], mb[:, 128:], jnp.zeros((2, 128), F32)], axis=0
        )


def inputs_grad(x, w, gain, dp_a, dp_b, gb_a, gb_b):
    rows = x.shape[0]
    block = pl.BlockSpec((1, 256, 256), lambda s: (s, 0, 0))
    quad = pl.BlockSpec((1, 4, 128, 256), lambda s: (s, 0, 0, 0))
    whole = lambda a: pl.BlockSpec(a.shape, lambda s: (0,) * a.ndim)

    def kernel(*refs):
        inputs_kernel(rows, *refs)

    return pl.pallas_call(
        kernel,
        grid=(rows,),
        in_specs=[block, whole(w), whole(gain), quad, quad, whole(gb_a), whole(gb_b)],
        out_specs=[block, pl.BlockSpec((8, 128), lambda s: (0, 0))],
        out_shape=[
            jax.ShapeDtypeStruct((rows, 256, 256), BF16),
            jax.ShapeDtypeStruct((8, 128), F32),
        ],
        scratch_shapes=[pltpu.VMEM((1, 256), F32), pltpu.VMEM((1, 256), F32)],
        compiler_params=pltpu.CompilerParams(vmem_limit_bytes=VMEM_LIMIT),
        cost_estimate=TINY,
        name="inputs_grad",
    )(x, w, gain, dp_a, dp_b, gb_a, gb_b)


def unpack_kernel(total_ref, dw_ref, dwo_ref, gb_ref, mg_ref, mb_ref, pg_ref, wb_ref, all_ref, main_ref):
    f = float(524288) ** (-0.5)
    fp = float(262144) ** (-0.5)
    all_ref[...] = total_ref[...].astype(F32)
    for g8 in range(320):
        at = 8 * (g8 % 5)
        main_ref[8 * g8 : 8 * g8 + 8, :] = all_ref[g8 // 5, at : at + 8, :] * f
    for side in range(2):
        lanes = slice(128 * side, 128 * side + 128)
        base = 1280 * side
        dw_ref[lanes, :] = main_ref[base : base + 1024, :].T
        dwo_ref[:, lanes] = main_ref[base + 1024 : base + 1280, :]
    tail = jnp.sum(all_ref[:, 40:56, :], axis=0)
    for n, ref in enumerate((gb_ref, mg_ref, mb_ref)):
        ref[...] = jnp.concatenate([tail[2 * n : 2 * n + 1], tail[2 * n + 1 : 2 * n + 2]], axis=1) * f
    pg_ref[...] = tail[6:7] * fp
    wb_ref[...] = (tail[8:16] * fp).T


def unpack(total):
    vector = jax.ShapeDtypeStruct((1, 256), F32)
    return pl.pallas_call(
        unpack_kernel,
        out_shape=[
            jax.ShapeDtypeStruct((256, 1024), F32),
            jax.ShapeDtypeStruct((256, 256), F32),
            vector, vector, vector,
            jax.ShapeDtypeStruct((1, 128), F32),
            jax.ShapeDtypeStruct((128, 8), F32),
        ],
        scratch_shapes=[pltpu.VMEM((64, 56, 128), F32), pltpu.VMEM((2560, 128), F32)],
        compiler_params=pltpu.CompilerParams(vmem_limit_bytes=VMEM_LIMIT),
        cost_estimate=TINY,
        name="unpack",
    )(total)


def pair_bias_kernel(pair_ref, gain_ref, w_ref, own_ref):
    wt = w_ref[...].astype(F32).T.astype(BF16)
    for i in range(4):
        for side in range(2):
            unit, _ = norm_rows(pair_ref[i, 128 * side : 128 * side + 128, :].astype(F32))
            both = mm(wt, (unit * gain_ref[...]).astype(BF16), NT)
            at = 8 * i + 4 * side
            own_ref[at : at + 4, :] = both[0:4]
            own_ref[32 + at : 36 + at, :] = both[4:8]


def pair_bias(pair, gain, w):
    return pl.pallas_call(
        pair_bias_kernel,
        out_shape=jax.ShapeDtypeStruct((64, 128), F32),
        compiler_params=pltpu.CompilerParams(vmem_limit_bytes=VMEM_LIMIT),
        cost_estimate=TINY,
        name="pair_bias",
    )(pair, gain, w)


def pair_grad_kernel(parts_ref, small_ref, pair_ref, gain_ref, w_ref, dpair_ref, block_ref, mine_ref):
    mine_ref[...] = jnp.sum(parts_ref[...].astype(F32), axis=0)
    wt = w_ref[...].astype(F32).T
    gain = gain_ref[...]
    d_wb = jnp.zeros((8, 128), F32)
    d_pg = jnp.zeros((1, 128), F32)
    high = lax.Precision.HIGHEST
    for i in range(4):
        for side in range(2):
            here = slice(128 * side, 128 * side + 128)
            at = 8 * i + 4 * side
            d_bias = jnp.concatenate([mine_ref[at : at + 4, :], mine_ref[32 + at : 36 + at, :]], axis=0)
            unit, inverse = norm_rows(pair_ref[i, here, :].astype(F32))
            normed = (unit * gain).astype(BF16).astype(F32)
            dpn = lax.dot_general(d_bias.T, wt, NN, precision=high, preferred_element_type=F32)
            d_wb += lax.dot_general(d_bias, normed, NN, precision=high, preferred_element_type=F32)
            d_pg += jnp.sum(unit * dpn, axis=0, keepdims=True)
            g = dpn * gain
            mean = jnp.mean(g, axis=-1, keepdims=True)
            cross = jnp.mean(g * unit, axis=-1, keepdims=True)
            dpair_ref[i, here, :] = (inverse * (g - mean - unit * cross)).astype(BF16)
    block_ref[0:40, :] = mine_ref[64:104, :]
    block_ref[40:48, :] = jnp.concatenate([small_ref[0:6, :], d_pg, small_ref[7:8, :]], axis=0)
    block_ref[48:56, :] = d_wb


def pair_grad(parts, small, pair, gain, w):
    return pl.pallas_call(
        pair_grad_kernel,
        out_shape=[
            jax.ShapeDtypeStruct((4, 256, 128), BF16),
            jax.ShapeDtypeStruct((56, 128), F32),
        ],
        scratch_shapes=[pltpu.VMEM((104, 128), F32)],
        compiler_params=pltpu.CompilerParams(vmem_limit_bytes=VMEM_LIMIT),
        cost_estimate=TINY,
        name="pair_grad",
    )(parts, small, pair, gain, w)


def exchange(blocks, axes):
    return lax.all_to_all(blocks, axes, 0, 0, tiled=True)


def spread(block, count, axes):
    return exchange(jnp.broadcast_to(block[None], (count,) + block.shape), axes)


def local(x, pair, adj, w, gbias, wo, gain, shift, pair_gain, pair_w):
    x, adj, pair = x[0], adj[0], pair[0]
    gain2, shift2 = gain.reshape(1, 256), shift.reshape(1, 256)
    pair_gain2 = pair_gain.reshape(1, 128)
    column = spread(pair_bias(pair, pair_gain2, pair_w), 8, "z")
    bias_a = spread(column[:, :32], 8, PLANE).reshape(2048, 128)
    *made, copies = project(x, adj, w, wo, gain2, shift2, gbias.reshape(1, 256), column)
    bias_b = exchange(copies, PLANE).reshape(2048, 128)

    dp_a, gb_a, send_a, grad_a = attend(bias_a, *made, adj, 0, None)
    dp_b, gb_b, send_b = attend(bias_b, *made, adj, 4, grad_a)
    dx, small = inputs_grad(x, w, gain2, dp_a, dp_b, gb_a, gb_b)

    sums = [
        jnp.sum(exchange(t.reshape(8, 8, -1, 128), PLANE).astype(F32), axis=0).astype(BF16)
        for t in (send_a, send_b)
    ]
    parts = exchange(jnp.concatenate(sums, axis=1), "z")
    dpair, block = pair_grad(parts, small, pair, pair_gain2, pair_w)
    block = block + lax.ppermute(block, "core", [(0, 1), (1, 0)])
    block = block + lax.ppermute(block, "x_lo", [(0, 1), (1, 0)])
    total = spread(spread(block.astype(BF16), 8, "z"), 8, PLANE).reshape(64, 56, 128)
    dw, dwo, gb, mg, mb, pg, wb = unpack(total)
    return (
        dx[None],
        dpair[None],
        dw,
        gb.reshape(256),
        dwo,
        mg.reshape(256),
        mb.reshape(256),
        pg.reshape(128),
        wb,
    )


def solution(mesh):
    fine = Mesh(mesh.devices.reshape(2, 2, 4, 8, 2), ("x_lo", "core", "y", "z", "x_hi"))
    split = P(("x_lo", "core"), AXIAL)
    return jax.shard_map(
        local,
        mesh=fine,
        in_specs=(split,) * 3 + (P(),) * 7,
        out_specs=(split, split) + (P(),) * 7,
        check_vma=False,
    )
```

time: 259 us -> 169 us (0.65)
  blocking collectives: 110 us -> 51.4 us
  waiting for transfers between devices: 54.3 us -> 27.5 us
  starting transfers between devices: 12.3 us -> 27.8 us
  between operations: 14.2 us -> 0.72 us
    all_gather x5 -> x0, blocking collectives: 82 us -> none  [the longest x3 44.8 us: local(): total = lax.all_gather(total, axis, tiled=True)]
    all_gather x2 -> x0, waiting for transfers between devices: 31.8 us -> none  [the longest x1 22.2 us: local(): bias = lax.all_gather(bias, axis, tiled=True)]
    all_to_all x2 -> x3, blocking collectives: 27.7 us -> 51.4 us  [exchange(): return lax.all_to_all(blocks, axes, 0, 0, tiled=True)]
    all_to_all x1 -> x5, starting transfers between devices: 10.7 us -> 26.4 us  [exchange(): return lax.all_to_all(blocks, axes, 0, 0, tiled=True)]
    all_to_all x1 -> x5, waiting for transfers between devices: 20.2 us -> 23.6 us  [exchange(): return lax.all_to_all(blocks, axes, 0, 0, tiled=True)]
    pallas_call x2 -> x6, Pallas kernels: 43.5 us -> 43.1 us  [the longest x2 26.6 us: attend(): pl.pallas_call(kernel, grid=(rows // 2,), in_specs=in_specs, out_specs=ou...]
  transfers between devices with their start and end apart: 4 -> 7, of which waited for: 4 -> 6; matrix products, arithmetic and copies ran while one was open for 1% -> 0% of each run, Pallas kernels for 8% -> 27%
where the time goes in v2:
time: 169 us; the launch traced here: 168 us
  Pallas kernels  53.5 us (32%)
  blocking collectives  51.4 us (30%)
  starting transfers between devices  27.8 us (16%)
  waiting for transfers between devices  27.5 us (16%)
  local copies, waits for them, and re-layouts  5.62 us (3%)
  other arithmetic  1.7 us (1%)
    all_to_all x3, blocking collectives, exchange(): return lax.all_to_all(blocks, axes, 0, 0, tiled=True)  51.4 us
    pallas_call x2, Pallas kernels, attend(): pl.pallas_call(kernel, grid=(rows // 2,), in_specs=in_specs, out_specs=ou...  26.6 us
    all_to_all x5, starting transfers between devices, exchange(): return lax.all_to_all(blocks, axes, 0, 0, tiled=True)  26.4 us
    all_to_all x5, waiting for transfers between devices, exchange(): return lax.all_to_all(blocks, axes, 0, 0, tiled=True)  23.6 us
    pallas_call x1, Pallas kernels, project(): pl.pallas_call(project_kernel, grid=(rows,), in_specs=[block, block, whol...  10.4 us
    pallas_call x1, Pallas kernels, inputs_grad(): pl.pallas_call(kernel, grid=(rows,), in_specs=[block, whole(w), whole(gai...  8.29 us
    unnamed x10, local copies, waits for them, and re-layouts  3.59 us
    pallas_call x1, Pallas kernels, pair_grad(): pl.pallas_call(pair_grad_kernel, out_shape=[jax.ShapeDtypeStruct((4, 256,...  3.47 us
  transfers between devices with their start and end apart: 7, of which 6 were waited for; matrix products, arithmetic and copies ran while one was open for 0% of the time, Pallas kernels for 27%

profile of v2, /device:TPU:2, one launch (start us, length us, event | category | flops | bytes accessed | tf_op | source)
XLA Modules:
  0.0 168.3 jit_solution(10243092039534776548)
XLA Ops:
  0.6 1.4 copy.19.w_ref
  2.0 2.1 %pair_bias.1 = f32[64,128]{1,0:T(8,128)} custom-call(bf16[4,256,128]{2,1,0:T(8,128)(2,1)} %bitcast.27, f32[1,128]{1,0:T(1,128)} %bitcast.32, bf16[128,8]{1,0:T(8,128)(2,1)} %copy.19.w_ref), custom_call_target="tpu_custom_call" | custom-call | flops 1000 | bytes 1000 | tf_op jit(solution)/shard_map/pair_bias/pallas_call | solution.py:363
  4.2 0.8 broadcast_in_dim.12
  5.0 20.1 %all_to_all.40.column_ref = f32[8,64,128]{2,1,0:T(8,128)S(1)} all-to-all(f32[8,64,128]{2,1,0:T(8,128)S(1)} %broadcast_in_dim.12), channel_id=1, replica_groups=mesh['x_lo'=2,'core'=2,'y'=4,'z'=8,'x_hi'=2] {'z'}, dimensions={0} | all-to-all | bytes 524288 | tf_op jit(solution)/shard_map/all_to_all | solution.py:413
  25.1 0.0 copy-start.2
  25.1 1.1 broadcast_in_dim.13
  26.2 6.0 %all-to-all-start.1 = ((f32[8,8,32,128]{3,2,1,0:T(8,128)}), f32[8,8,32,128]{3,2,1,0:T(8,128)S(1)}, u32[]{:S(2)}, u32[]{:S(2)}) async-start(f32[8,8,32,128]{3,2,1,0:T(8,128)} %broadcast_in_dim.13), calls=%async_computation.1 | async-start | bytes 2097152 | tf_op jit(solution)/shard_map/all_to_all | solution.py:413
  32.2 0.0 copy-done.2
  32.3 10.4 %project.1 = (bf16[8,256,256]{2,1,0:T(8,128)(2,1)}, bf16[8,256,256]{2,1,0:T(8,128)(2,1)}, bf16[8,256,256]{2,1,0:T(8,128)(2,1)}, bf16[8,256,256]{2,1,0:T(8,128)(2...) custom-call(bf16[8,256,256]{2,1,0:T(8,128)(2,1)} %bitcast.21, ...), custom_call_target="tpu_custom_call" | custom-call | flops 1000 | bytes 1000 | tf_op jit(solution)/shard_map/project/pallas_call | solution.py:67
  42.6 5.1 %all-to-all-done.1 = f32[8,8,32,128]{3,2,1,0:T(8,128)S(1)} async-done(((f32[8,8,32,128]{3,2,1,0:T(8,128)}), f32[8,8,32,128]{3,2,1,0:T(8,128)S(1)}, u32[]{:S(2)}, u32[]{:S(2)}) %all-to-all-start.1) | async-done | bytes 1048608 | tf_op jit(solution)/shard_map/all_to_all | solution.py:413
  47.7 0.0 copy-start.1
  47.7 3.6 %all-to-all-start.2 = ((f32[8,256,128]{2,1,0:T(8,128)}), f32[8,256,128]{2,1,0:T(8,128)S(1)}, u32[]{:S(2)}, u32[]{:S(2)}) async-start(f32[8,256,128]{2,1,0:T(8,128)} %get-tuple-element.47), calls=%async_computation.2 | async-start | bytes 2097152 | tf_op jit(solution)/shard_map/all_to_all | solution.py:413
  51.3 0.0 copy-done.1
  51.3 13.2 %attend.2 = (bf16[8,4,128,256]{3,2,1,0:T(8,128)(2,1)}, f32[128,128]{1,0:T(8,128)}, bf16[64,32,128]{2,1,0:T(8,128)(2,1)}, f32[2,640,128]{2,1,0:T(8,128)}) custom-call(f32[2048,128]{1,0:T(8,128)} %bitcast.24, bf16[8,256,256]{2,1,0:T(8,128)(2,1)} %get-tuple-element.37.refs_1_, bf16[8,256,256]{2,1,0:T(8,128)(2,1)} %get-tuple-element.38.refs_2_, ...), custom_call_target="tpu_custom_call" | custom-call | flops 1000 | bytes 1000 | tf_op jit(solution)/shard_map/attend/pallas_call | solution.py:245
  64.5 1.7 all-to-all-done.2
  66.2 0.0 copy-start
  66.2 5.5 %all-to-all-start.3 = ((bf16[8,8,32,128]{3,2,1,0:T(8,128)(2,1)}), bf16[8,8,32,128]{3,2,1,0:T(8,128)(2,1)S(1)}, u32[]{:S(2)}, u32[]{:S(2)}) async-start(bf16[8,8,32,128]{3,2,1,0:T(8,128)(2,1)} %bitcast.29), calls=%async_computation.3 | async-start | bytes 1048576 | tf_op jit(solution)/shard_map/all_to_all | solution.py:413
  71.6 0.0 copy-done
  71.6 13.5 %attend.3 = (bf16[8,4,128,256]{3,2,1,0:T(8,128)(2,1)}, f32[128,128]{1,0:T(8,128)}, bf16[64,72,128]{2,1,0:T(8,128)(2,1)}) custom-call(f32[2048,128]{1,0:T(8,128)} %bitcast.23, bf16[8,256,256]{2,1,0:T(8,128)(2,1)} %get-tuple-element.37.refs_1_, bf16[8,256,256]{2,1,0:T(8,128)(2,1)} %get-tuple-element.38.refs_2_, ...), custom_call_target="tpu_custom_call" | custom-call | flops 1000 | bytes 1000 | tf_op jit(solution)/shard_map/attend/pallas_call | solution.py:245
  85.1 0.0 all-to-all-done.3
  85.1 7.2 %all-to-all-start.4 = ((bf16[8,8,72,128]{3,2,1,0:T(8,128)(2,1)}), bf16[8,8,72,128]{3,2,1,0:T(8,128)(2,1)S(1)}, u32[]{:S(2)}, u32[]{:S(2)}) async-start(bf16[8,8,72,128]{3,2,1,0:T(8,128)(2,1)} %bitcast.26), calls=%async_computation.4 | async-start | bytes 2359296 | tf_op jit(solution)/shard_map/all_to_all | solution.py:413
  92.3 0.1 reduce_sum.24
  92.4 15.2 %all-to-all-done.4 = bf16[8,8,72,128]{3,2,1,0:T(8,128)(2,1)S(1)} async-done(((bf16[8,8,72,128]{3,2,1,0:T(8,128)(2,1)}), bf16[8,8,72,128]{3,2,1,0:T(8,128)(2,1)S(1)}, u32[]{:S(2)}, u32[]{:S(2)}) %all-to-all-start.4) | async-done | bytes 1179680 | tf_op jit(solution)/shard_map/all_to_all | solution.py:413
  107.5 0.2 reduce_sum.25
  107.7 0.7 pad_maximum_fusion
  108.4 4.2 %all-to-all-start.5 = ((bf16[8,104,128]{2,1,0:T(8,128)(2,1)}), bf16[8,104,128]{2,1,0:T(8,128)(2,1)S(1)}, u32[]{:S(2)}, u32[]{:S(2)}) async-start(bf16[8,104,128]{2,1,0:T(8,128)(2,1)} %pad_maximum_fusion), calls=%async_computation.5 | async-start | bytes 425984 | tf_op jit(solution)/shard_map/all_to_all | solution.py:413
  112.6 8.3 %inputs_grad.1 = (bf16[8,256,256]{2,1,0:T(8,128)(2,1)}, f32[8,128]{1,0:T(8,128)}) custom-call(bf16[8,256,256]{2,1,0:T(8,128)(2,1)} %bitcast.22, bf16[256,1024]{1,0:T(8,128)(2,1)} %refs_1_.1, f32[1,256]{1,0:T(1,128)} %bitcast.31, bf16[8,4,128,256]{3,2,1,0:T(8,128)(2,1)} %get-tuple-element.46.refs_3_, bf16[8,4,128,256]{3,2,1,0:T(8,128)(2,1)} %get-tuple-element.49.refs_4_, ...), custom_call_target="tpu_custom_call" | custom-call | flops 1000 | bytes 1000 | tf_op jit(solution)/shard_map/inputs_grad/pallas_call | solution.py:298
  120.9 1.7 all-to-all-done.5.parts_ref
  122.5 0.0 copy-start.3
  122.5 0.7 copy-done.3
  123.2 3.5 %pair_grad.1 = (bf16[4,256,128]{2,1,0:T(8,128)(2,1)}, f32[56,128]{1,0:T(8,128)}) custom-call(bf16[8,104,128]{2,1,0:T(8,128)(2,1)} %copy-done.3, f32[8,128]{1,0:T(8,128)} %get-tuple-element.55.small_ref, bf16[4,256,128]{2,1,0:T(8,128)(2,1)} %bitcast.28, f32[1,128]{1,0:T(1,128)} %bitcast.33, bf16[128,8]{1,0:T(8,128)(2,1)} %copy.19.w_ref), custom_call_target="tpu_custom_call" | custom-call | flops 1000 | bytes 1000 | tf_op jit(solution)/shard_map/pair_grad/pallas_call | solution.py:399
  126.7 0.0 collective-permute-start
  126.7 1.4 collective-permute-done
  128.1 0.8 add.6
  128.8 1.4 collective-permute-start.1
  130.3 2.5 %collective-permute-done.1 = f32[56,128]{1,0:T(8,128)S(1)} collective-permute-done((f32[56,128]{1,0:T(8,128)S(1)}, f32[56,128]{1,0:T(8,128)S(1)}, u32[]{:S(2)}, u32[]{:S(2)}) %collective-permute-start.1) | collective-permute-done | bytes 28704 | tf_op jit(solution)/shard_map/ppermute | solution.py:440
  132.7 14.2 %all_to_all.41 = bf16[8,56,128]{2,1,0:T(8,128)(2,1)S(1)} all-to-all(bf16[8,56,128]{2,1,0:T(8,128)(2,1)S(1)} %broadcast_in_dim.16), channel_id=1, replica_groups=mesh['x_lo'=2,'core'=2,'y'=4,'z'=8,'x_hi'=2] {'z'}, dimensions={0} | all-to-all | bytes 229376 | tf_op jit(solution)/shard_map/all_to_all | solution.py:413
  147.0 0.1 broadcast_in_dim.17
  147.1 17.1 %all_to_all.42 = bf16[8,8,56,128]{3,2,1,0:T(8,128)(2,1)} all-to-all(bf16[8,8,56,128]{3,2,1,0:T(8,128)(2,1)S(1)} %broadcast_in_dim.17), channel_id=1, replica_groups=mesh['x_lo'=2,'core'=2,'y'=4,'z'=8,'x_hi'=2] {'y','x_hi'}, dimensions={0} | all-to-all | bytes 1835008 | tf_op jit(solution)/shard_map/all_to_all | solution.py:413
  164.2 2.6 %unpack.1 = (f32[256,1024]{1,0:T(8,128)}, f32[256,256]{1,0:T(8,128)}, f32[1,256]{1,0:T(1,128)}, f32[1,256]{1,0:T(1,128)}, f32[1,256]{1,0:T(1,128)}, /*index=5*/f32[1,128]{1,0:T(1,128)}, f32[128,8]{1,0:T(8,128)}) custom-call(bf16[64,56,128]{2,1,0:T(8,128)(2,1)} %bitcast.25), custom_call_target="tpu_custom_call" | custom-call | flops 1000 | bytes 1000 | tf_op jit(solution)/shard_map/unpack/pallas_call | solution.py:335
  166.8 1.5 copy.21
  (3 shorter events, 0.0 us)
Async XLA Ops:
  25.1 7.1 %copy-start.2 = (f32[8,64,128]{2,1,0:T(8,128)}, f32[8,64,128]{2,1,0:T(8,128)S(1)}, u32[]{:S(2)}) copy-start(f32[8,64,128]{2,1,0:T(8,128)S(1)} %all_to_all.40.column_ref) | copy-start | bytes 786436
  26.2 21.5 %all-to-all-start.1 = ((f32[8,8,32,128]{3,2,1,0:T(8,128)}), f32[8,8,32,128]{3,2,1,0:T(8,128)S(1)}, u32[]{:S(2)}, u32[]{:S(2)}) async-start(f32[8,8,32,128]{3,2,1,0:T(8,128)} %broadcast_in_dim.13), calls=%async_computation.1 | async-start | bytes 2097152 | tf_op jit(solution)/shard_map/all_to_all | solution.py:413
  47.7 3.6 %copy-start.1 = (f32[8,8,32,128]{3,2,1,0:T(8,128)}, f32[8,8,32,128]{3,2,1,0:T(8,128)S(1)}, u32[]{:S(2)}) copy-start(f32[8,8,32,128]{3,2,1,0:T(8,128)S(1)} %all-to-all-done.1) | copy-start | bytes 3145732
  47.7 18.4 %all-to-all-start.2 = ((f32[8,256,128]{2,1,0:T(8,128)}), f32[8,256,128]{2,1,0:T(8,128)S(1)}, u32[]{:S(2)}, u32[]{:S(2)}) async-start(f32[8,256,128]{2,1,0:T(8,128)} %get-tuple-element.47), calls=%async_computation.2 | async-start | bytes 2097152 | tf_op jit(solution)/shard_map/all_to_all | solution.py:413
  66.2 5.5 %copy-start = (f32[8,256,128]{2,1,0:T(8,128)}, f32[8,256,128]{2,1,0:T(8,128)S(1)}, u32[]{:S(2)}) copy-start(f32[8,256,128]{2,1,0:T(8,128)S(1)} %all-to-all-done.2) | copy-start | bytes 3145732
  66.2 18.9 %all-to-all-start.3 = ((bf16[8,8,32,128]{3,2,1,0:T(8,128)(2,1)}), bf16[8,8,32,128]{3,2,1,0:T(8,128)(2,1)S(1)}, u32[]{:S(2)}, u32[]{:S(2)}) async-start(bf16[8,8,32,128]{3,2,1,0:T(8,128)(2,1)} %bitcast.29), calls=%async_computation.3 | async-start | bytes 1048576 | tf_op jit(solution)/shard_map/all_to_all | solution.py:413
  85.1 22.4 %all-to-all-start.4 = ((bf16[8,8,72,128]{3,2,1,0:T(8,128)(2,1)}), bf16[8,8,72,128]{3,2,1,0:T(8,128)(2,1)S(1)}, u32[]{:S(2)}, u32[]{:S(2)}) async-start(bf16[8,8,72,128]{3,2,1,0:T(8,128)(2,1)} %bitcast.26), calls=%async_computation.4 | async-start | bytes 2359296 | tf_op jit(solution)/shard_map/all_to_all | solution.py:413
  108.4 14.1 %all-to-all-start.5 = ((bf16[8,104,128]{2,1,0:T(8,128)(2,1)}), bf16[8,104,128]{2,1,0:T(8,128)(2,1)S(1)}, u32[]{:S(2)}, u32[]{:S(2)}) async-start(bf16[8,104,128]{2,1,0:T(8,128)(2,1)} %pad_maximum_fusion), calls=%async_computation.5 | async-start | bytes 425984 | tf_op jit(solution)/shard_map/all_to_all | solution.py:413
  122.5 0.7 copy-start.3
  126.7 1.4 collective-permute-start
  128.8 3.9 %collective-permute-start.1 = (f32[56,128]{1,0:T(8,128)S(1)}, f32[56,128]{1,0:T(8,128)S(1)}, u32[]{:S(2)}, u32[]{:S(2)}) collective-permute-start(f32[56,128]{1,0:T(8,128)S(1)} %add.6), channel_id=1, source_target_pairs={{0,128},{128,0},{1,129},{129,1},{2,130},{130,2},{3,131},{131,3},{4... | collective-permute-start | bytes 86024 | tf_op jit(solution)/shard_map/ppermute | solution.py:440

commit v3 on v2

--- a/solution.py
+++ b/solution.py
@@ -12,6 +12,19 @@
 PLANE = ("y", "x_hi")
 SENT = [(y * 2 + x) * 8 + z for y in range(4) for z in range(8) for x in range(2)]
 TINY = pl.CostEstimate(flops=1000, bytes_accessed=1000, transcendentals=0)
+FIRST = [(side, 8 * n) for side in range(2) for n in range(64)]
+SECOND = [(0, side, 8 * n) for side in range(2) for n in range(64, 80)]
+SECOND += [(1, side, 8 * n) for side in range(2) for n in range(80)]
+
+
+def packed_row(chunk, side, row):
+    return 1280 * side + 256 * (row // 128) + 128 * chunk + row % 128
+
+
+GROUPS = [
+    [packed_row(0, *g) for g in FIRST[2 * d : 2 * d + 2]] + [packed_row(*g) for g in SECOND[3 * d : 3 * d + 3]]
+    for d in range(64)
+]
 VMEM_LIMIT = 56 * 1024 * 1024
 
 NN = (((1,), (0,)), ((), ()))
@@ -84,7 +97,7 @@
     if last:
         other_ref, dp_ref, gb_ref, send_ref, bt_ref, acc_ref, out_ref, w_ref, stage_ref = refs
     else:
-        dp_ref, gb_ref, send_ref, grad_ref, bt_ref, acc_ref, out_ref, w_ref = refs
+        dp_ref, gb_ref, send_ref, grad_ref, bt_ref, acc_ref, out_ref, w_ref, stage_ref = refs
     step = pl.program_id(0)
     width = 32 * heads
 
@@ -183,27 +196,23 @@
             for side in range(2):
                 part = acc_ref[h, 128 * side : 128 * side + 128, :]
                 out_ref[pl.ds(side * heads + h, 256, stride=2 * heads), :] = part.T
+        for natural, sent in enumerate(SENT):
+            stage_ref[sent, 0:32, :] = out_ref[32 * natural : 32 * natural + 32, :]
         if not last:
-            for natural, sent in enumerate(SENT):
-                send_ref[sent] = out_ref[32 * natural : 32 * natural + 32, :].astype(BF16)
+            for n, (side, row) in enumerate(FIRST):
+                to = 32 + 8 * (n % 2)
+                stage_ref[n // 2, to : to + 8, :] = w_ref[row : row + 8, 128 * side : 128 * side + 128]
             for side in range(2):
-                grad_ref[side] = w_ref[:, 128 * side : 128 * side + 128]
+                grad_ref[side] = w_ref[512:640, 128 * side : 128 * side + 128]
         else:
-            for natural, sent in enumerate(SENT):
-                stage_ref[sent, 0:32, :] = out_ref[32 * natural : 32 * natural + 32, :]
-            for side in range(2):
-                for b in range(5):
-                    for c in range(2):
-                        for r in range(16):
-                            g8 = 160 * side + 32 * b + 16 * c + r
-                            at = 128 * b + 8 * r
-                            if c:
-                                piece = w_ref[at : at + 8, 128 * side : 128 * side + 128]
-                            else:
-                                piece = other_ref[side, at : at + 8, :]
-                            to = 32 + 8 * (g8 % 5)
-                            stage_ref[g8 // 5, to : to + 8, :] = piece
-            send_ref[...] = stage_ref[...].astype(BF16)
+            for n, (c, side, row) in enumerate(SECOND):
+                to = 32 + 8 * (n % 3)
+                if c:
+                    piece = w_ref[row : row + 8, 128 * side : 128 * side + 128]
+                else:
+                    piece = other_ref[side, row - 512 : row - 504, :]
+                stage_ref[n // 3, to : to + 8, :] = piece
+        send_ref[...] = stage_ref[...].astype(BF16)
 
 
 def attend(bias, qt, kt, vt, k, v, gt, dgt, dat, xn, adj, first, other):
@@ -231,17 +240,17 @@
         pltpu.VMEM((5 * width, 256), F32),
     ]
     operands = [bias, qt, kt, vt, k, v, gt, dgt, dat, xn, adj]
+    height = 8 * heads + (24 if last else 16)
+    out_specs.append(pl.BlockSpec((64, height, 128), lambda s: (0, 0, 0)))
+    out_shape.append(jax.ShapeDtypeStruct((64, height, 128), BF16))
+    scratch.append(pltpu.VMEM((64, height, 128), F32))
+    rest = pl.BlockSpec((2, width, 128), lambda s: (0, 0, 0))
     if last:
-        in_specs.append(pl.BlockSpec((2, 5 * width, 128), lambda s: (0, 0, 0)))
-        out_specs.append(pl.BlockSpec((64, 72, 128), lambda s: (0, 0, 0)))
-        out_shape.append(jax.ShapeDtypeStruct((64, 72, 128), BF16))
-        scratch.append(pltpu.VMEM((64, 72, 128), F32))
+        in_specs.append(rest)
         operands.append(other)
     else:
-        out_specs.append(pl.BlockSpec((64, 8 * heads, 128), lambda s: (0, 0, 0)))
-        out_shape.append(jax.ShapeDtypeStruct((64, 8 * heads, 128), BF16))
-        out_specs.append(pl.BlockSpec((2, 5 * width, 128), lambda s: (0, 0, 0)))
-        out_shape.append(jax.ShapeDtypeStruct((2, 5 * width, 128), F32))
+        out_specs.append(rest)
+        out_shape.append(jax.ShapeDtypeStruct((2, width, 128), F32))
     return pl.pallas_call(
         kernel,
         grid=(rows // 2,),
@@ -315,19 +324,20 @@
     f = float(524288) ** (-0.5)
     fp = float(262144) ** (-0.5)
     all_ref[...] = total_ref[...].astype(F32)
-    for g8 in range(320):
-        at = 8 * (g8 % 5)
-        main_ref[8 * g8 : 8 * g8 + 8, :] = all_ref[g8 // 5, at : at + 8, :] * f
+    for d in range(64):
+        for k, row in enumerate(GROUPS[d]):
+            at = 40 * (d % 8) + 8 * k
+            main_ref[row : row + 8, :] = all_ref[d // 8, at : at + 8, :] * f
     for side in range(2):
         lanes = slice(128 * side, 128 * side + 128)
         base = 1280 * side
         dw_ref[lanes, :] = main_ref[base : base + 1024, :].T
         dwo_ref[:, lanes] = main_ref[base + 1024 : base + 1280, :]
-    tail = jnp.sum(all_ref[:, 40:56, :], axis=0)
+    tail = jnp.sum(all_ref[:, 320:336, :], axis=0)
     for n, ref in enumerate((gb_ref, mg_ref, mb_ref)):
         ref[...] = jnp.concatenate([tail[2 * n : 2 * n + 1], tail[2 * n + 1 : 2 * n + 2]], axis=1) * f
     pg_ref[...] = tail[6:7] * fp
-    wb_ref[...] = (tail[8:16] * fp).T
+    wb_ref[...] = tail[8:16] * fp
 
 
 def unpack(total):
@@ -339,52 +349,55 @@
             jax.ShapeDtypeStruct((256, 256), F32),
             vector, vector, vector,
             jax.ShapeDtypeStruct((1, 128), F32),
-            jax.ShapeDtypeStruct((128, 8), F32),
+            jax.ShapeDtypeStruct((8, 128), F32),
         ],
-        scratch_shapes=[pltpu.VMEM((64, 56, 128), F32), pltpu.VMEM((2560, 128), F32)],
+        scratch_shapes=[pltpu.VMEM((8, 336, 128), F32), pltpu.VMEM((2560, 128), F32)],
         compiler_params=pltpu.CompilerParams(vmem_limit_bytes=VMEM_LIMIT),
         cost_estimate=TINY,
         name="unpack",
     )(total)
 
 
-def pair_bias_kernel(pair_ref, gain_ref, w_ref, own_ref):
-    wt = w_ref[...].astype(F32).T.astype(BF16)
+def pair_bias_kernel(pair_ref, gain_ref, wt_ref, own_ref):
+    wt = wt_ref[...]
     for i in range(4):
         for side in range(2):
             unit, _ = norm_rows(pair_ref[i, 128 * side : 128 * side + 128, :].astype(F32))
             both = mm(wt, (unit * gain_ref[...]).astype(BF16), NT)
             at = 8 * i + 4 * side
-            own_ref[at : at + 4, :] = both[0:4]
-            own_ref[32 + at : 36 + at, :] = both[4:8]
-
-
-def pair_bias(pair, gain, w):
+            for r in range(8):
+                own_ref[r, at : at + 4, :] = both[0:4]
+                own_ref[r, 32 + at : 36 + at, :] = both[4:8]
+
+
+def pair_bias(pair, gain, wt):
     return pl.pallas_call(
         pair_bias_kernel,
-        out_shape=jax.ShapeDtypeStruct((64, 128), F32),
+        out_shape=jax.ShapeDtypeStruct((8, 64, 128), F32),
         compiler_params=pltpu.CompilerParams(vmem_limit_bytes=VMEM_LIMIT),
         cost_estimate=TINY,
         name="pair_bias",
-    )(pair, gain, w)
-
-
-def pair_grad_kernel(parts_ref, small_ref, pair_ref, gain_ref, w_ref, dpair_ref, block_ref, mine_ref):
+    )(pair, gain, wt)
+
+
+def pair_grad_kernel(parts_ref, small_ref, pair_ref, gain_ref, wt_ref, dpair_ref, block_ref, mine_ref):
     mine_ref[...] = jnp.sum(parts_ref[...].astype(F32), axis=0)
-    wt = w_ref[...].astype(F32).T
+    wt = jnp.concatenate([wt_ref[...].astype(F32)] * 2, axis=0).astype(BF16)
     gain = gain_ref[...]
     d_wb = jnp.zeros((8, 128), F32)
     d_pg = jnp.zeros((1, 128), F32)
-    high = lax.Precision.HIGHEST
     for i in range(4):
         for side in range(2):
             here = slice(128 * side, 128 * side + 128)
             at = 8 * i + 4 * side
             d_bias = jnp.concatenate([mine_ref[at : at + 4, :], mine_ref[32 + at : 36 + at, :]], axis=0)
+            high = d_bias.astype(BF16).astype(F32)
+            pieces = jnp.concatenate([high, d_bias - high], axis=0)
             unit, inverse = norm_rows(pair_ref[i, here, :].astype(F32))
-            normed = (unit * gain).astype(BF16).astype(F32)
-            dpn = lax.dot_general(d_bias.T, wt, NN, precision=high, preferred_element_type=F32)
-            d_wb += lax.dot_general(d_bias, normed, NN, precision=high, preferred_element_type=F32)
+            normed = (unit * gain).astype(BF16)
+            dpn = mm(pieces.T.astype(BF16), wt)
+            both = mm(pieces.astype(BF16), normed)
+            d_wb += both[0:8] + both[8:16]
             d_pg += jnp.sum(unit * dpn, axis=0, keepdims=True)
             g = dpn * gain
             mean = jnp.mean(g, axis=-1, keepdims=True)
@@ -395,7 +408,7 @@
     block_ref[48:56, :] = d_wb
 
 
-def pair_grad(parts, small, pair, gain, w):
+def pair_grad(parts, small, pair, gain, wt):
     return pl.pallas_call(
         pair_grad_kernel,
         out_shape=[
@@ -406,7 +419,7 @@
         compiler_params=pltpu.CompilerParams(vmem_limit_bytes=VMEM_LIMIT),
         cost_estimate=TINY,
         name="pair_grad",
-    )(parts, small, pair, gain, w)
+    )(parts, small, pair, gain, wt)
 
 
 def exchange(blocks, axes):
@@ -421,7 +434,8 @@
     x, adj, pair = x[0], adj[0], pair[0]
     gain2, shift2 = gain.reshape(1, 256), shift.reshape(1, 256)
     pair_gain2 = pair_gain.reshape(1, 128)
-    column = spread(pair_bias(pair, pair_gain2, pair_w), 8, "z")
+    pair_wt = pair_w.T
+    column = exchange(pair_bias(pair, pair_gain2, pair_wt), "z")
     bias_a = spread(column[:, :32], 8, PLANE).reshape(2048, 128)
     *made, copies = project(x, adj, w, wo, gain2, shift2, gbias.reshape(1, 256), column)
     bias_b = exchange(copies, PLANE).reshape(2048, 128)
@@ -434,11 +448,16 @@
         jnp.sum(exchange(t.reshape(8, 8, -1, 128), PLANE).astype(F32), axis=0).astype(BF16)
         for t in (send_a, send_b)
     ]
-    parts = exchange(jnp.concatenate(sums, axis=1), "z")
-    dpair, block = pair_grad(parts, small, pair, pair_gain2, pair_w)
-    block = block + lax.ppermute(block, "core", [(0, 1), (1, 0)])
-    block = block + lax.ppermute(block, "x_lo", [(0, 1), (1, 0)])
-    total = spread(spread(block.astype(BF16), 8, "z"), 8, PLANE).reshape(64, 56, 128)
+    order = [sums[0][:, :32], sums[1][:, :32], sums[0][:, 32:], sums[1][:, 32:]]
+    parts = exchange(jnp.concatenate(order, axis=1), "z")
+    dpair, block = pair_grad(parts, small, pair, pair_gain2, pair_wt)
+    others = [
+        lax.ppermute(block, ("x_lo", "core"), [(n, n ^ flip) for n in range(4)]) for flip in (1, 2, 3)
+    ]
+    block = (block + others[0]) + (others[1] + others[2])
+    line = spread(block.astype(BF16), 8, "z")
+    tail = jnp.sum(line[:, 40:].astype(F32), axis=0).astype(BF16)
+    total = spread(jnp.concatenate([line[:, :40].reshape(320, 128), tail], axis=0), 8, PLANE)
     dw, dwo, gb, mg, mb, pg, wb = unpack(total)
     return (
         dx[None],
@@ -449,7 +468,7 @@
         mg.reshape(256),
         mb.reshape(256),
         pg.reshape(128),
-        wb,
+        wb.T,
     )
 
 

time: 169 us -> 160 us (0.947)
  waiting for transfers between devices: 27.5 us -> 23 us
  local copies, waits for them, and re-layouts: 5.62 us -> 1.94 us
    unnamed x10 -> x8, local copies, waits for them, and re-layouts: 3.59 us -> 0.69 us
    all_to_all x5, waiting for transfers between devices: 23.6 us -> 20.8 us  [exchange(): return lax.all_to_all(blocks, axes, 0, 0, tiled=True)]
    ppermute x2 -> x3, waiting for transfers between devices: 3.87 us -> 2.25 us  [local(): lax.ppermute(block, ('x_lo', 'core'), [(n, n ^ flip) for n in range(4)])]
  transfers between devices with their start and end apart: 7 -> 8, of which waited for: 6 -> 6; matrix products, arithmetic and copies ran while one was open for 0% -> 0% of each run, Pallas kernels for 27% -> 28%
where the time goes in v3:
time: 160 us; the launch traced here: 159 us
  Pallas kernels  52.9 us (33%)
  blocking collectives  50.6 us (32%)
  starting transfers between devices  28.2 us (18%)
  waiting for transfers between devices  23 us (14%)
  local copies, waits for them, and re-layouts  1.94 us (1%)
  other arithmetic  1.72 us (1%)
    all_to_all x3, blocking collectives, exchange(): return lax.all_to_all(blocks, axes, 0, 0, tiled=True)  50.6 us
    all_to_all x5, starting transfers between devices, exchange(): return lax.all_to_all(blocks, axes, 0, 0, tiled=True)  26.4 us
    pallas_call x2, Pallas kernels, attend(): pl.pallas_call(kernel, grid=(rows // 2,), in_specs=in_specs, out_specs=ou...  26.2 us
    all_to_all x5, waiting for transfers between devices, exchange(): return lax.all_to_all(blocks, axes, 0, 0, tiled=True)  20.8 us
    pallas_call x1, Pallas kernels, project(): pl.pallas_call(project_kernel, grid=(rows,), in_specs=[block, block, whol...  10.3 us
    pallas_call x1, Pallas kernels, inputs_grad(): pl.pallas_call(kernel, grid=(rows,), in_specs=[block, whole(w), whole(gai...  8.29 us
    pallas_call x1, Pallas kernels, pair_grad(): pl.pallas_call(pair_grad_kernel, out_shape=[jax.ShapeDtypeStruct((4, 256,...  3.4 us
  transfers between devices with their start and end apart: 8, of which 6 were waited for; matrix products, arithmetic and copies ran while one was open for 0% of the time, Pallas kernels for 28%

profile of v3, /device:TPU:2, one launch (start us, length us, event | category | flops | bytes accessed | tf_op | source)
XLA Modules:
  0.0 159.3 jit_solution(8265032818476306813)
XLA Ops:
  0.6 2.2 %pair_bias.1 = f32[8,64,128]{2,1,0:T(8,128)} custom-call(bf16[4,256,128]{2,1,0:T(8,128)(2,1)} %bitcast.27, f32[1,128]{1,0:T(1,128)} %bitcast.36, bf16[8,128]{1,0:T(8,128)(2,1)} %bitcast.32), custom_call_target="tpu_custom_call" | custom-call | flops 1000 | bytes 1000 | tf_op jit(solution)/shard_map/pair_bias/pallas_call | solution.py:374
  2.9 20.3 %all_to_all.40.column_ref = f32[8,64,128]{2,1,0:T(8,128)S(1)} all-to-all(f32[8,64,128]{2,1,0:T(8,128)} %pair_bias.1), channel_id=1, replica_groups=mesh['x_lo'=2,'core'=2,'y'=4,'z'=8,'x_hi'=2] {'z'}, dimensions={0} | all-to-all | bytes 524288 | tf_op jit(solution)/shard_map/all_to_all | solution.py:426
  23.2 0.0 copy-start.2
  23.2 1.1 broadcast_in_dim.10
  24.3 6.0 %all-to-all-start.1 = ((f32[8,8,32,128]{3,2,1,0:T(8,128)}), f32[8,8,32,128]{3,2,1,0:T(8,128)S(1)}, u32[]{:S(2)}, u32[]{:S(2)}) async-start(f32[8,8,32,128]{3,2,1,0:T(8,128)} %broadcast_in_dim.10), calls=%async_computation.1 | async-start | bytes 2097152 | tf_op jit(solution)/shard_map/all_to_all | solution.py:426
  30.3 0.0 copy-done.2
  30.3 10.3 %project.1 = (bf16[8,256,256]{2,1,0:T(8,128)(2,1)}, bf16[8,256,256]{2,1,0:T(8,128)(2,1)}, bf16[8,256,256]{2,1,0:T(8,128)(2,1)}, bf16[8,256,256]{2,1,0:T(8,128)(2...) custom-call(bf16[8,256,256]{2,1,0:T(8,128)(2,1)} %bitcast.23, ...), custom_call_target="tpu_custom_call" | custom-call | flops 1000 | bytes 1000 | tf_op jit(solution)/shard_map/project/pallas_call | solution.py:80
  40.7 5.1 %all-to-all-done.1 = f32[8,8,32,128]{3,2,1,0:T(8,128)S(1)} async-done(((f32[8,8,32,128]{3,2,1,0:T(8,128)}), f32[8,8,32,128]{3,2,1,0:T(8,128)S(1)}, u32[]{:S(2)}, u32[]{:S(2)}) %all-to-all-start.1) | async-done | bytes 1048608 | tf_op jit(solution)/shard_map/all_to_all | solution.py:426
  45.8 0.0 copy-start.1
  45.8 3.6 %all-to-all-start.2 = ((f32[8,256,128]{2,1,0:T(8,128)}), f32[8,256,128]{2,1,0:T(8,128)S(1)}, u32[]{:S(2)}, u32[]{:S(2)}) async-start(f32[8,256,128]{2,1,0:T(8,128)} %get-tuple-element.47), calls=%async_computation.2 | async-start | bytes 2097152 | tf_op jit(solution)/shard_map/all_to_all | solution.py:426
  49.4 0.0 copy-done.1
  49.4 13.1 %attend.2 = (bf16[8,4,128,256]{3,2,1,0:T(8,128)(2,1)}, f32[128,128]{1,0:T(8,128)}, bf16[64,48,128]{2,1,0:T(8,128)(2,1)}, f32[2,128,128]{2,1,0:T(8,128)}) custom-call(f32[2048,128]{1,0:T(8,128)} %bitcast.26, bf16[8,256,256]{2,1,0:T(8,128)(2,1)} %get-tuple-element.37.refs_1_, bf16[8,256,256]{2,1,0:T(8,128)(2,1)} %get-tuple-element.38.refs_2_, ...), custom_call_target="tpu_custom_call" | custom-call | flops 1000 | bytes 1000 | tf_op jit(solution)/shard_map/attend/pallas_call | solution.py:254
  62.5 1.8 %all-to-all-done.2 = f32[8,256,128]{2,1,0:T(8,128)S(1)} async-done(((f32[8,256,128]{2,1,0:T(8,128)}), f32[8,256,128]{2,1,0:T(8,128)S(1)}, u32[]{:S(2)}, u32[]{:S(2)}) %all-to-all-start.2) | async-done | bytes 1048608 | tf_op jit(solution)/shard_map/all_to_all | solution.py:426
  64.2 0.0 copy-start
  64.3 5.4 %all-to-all-start.3 = ((bf16[8,8,48,128]{3,2,1,0:T(8,128)(2,1)}), bf16[8,8,48,128]{3,2,1,0:T(8,128)(2,1)S(1)}, u32[]{:S(2)}, u32[]{:S(2)}) async-start(bf16[8,8,48,128]{3,2,1,0:T(8,128)(2,1)} %bitcast.30), calls=%async_computation.3 | async-start | bytes 1572864 | tf_op jit(solution)/shard_map/all_to_all | solution.py:426
  69.6 0.0 copy-done
  69.6 13.1 %attend.3 = (bf16[8,4,128,256]{3,2,1,0:T(8,128)(2,1)}, f32[128,128]{1,0:T(8,128)}, bf16[64,56,128]{2,1,0:T(8,128)(2,1)}) custom-call(f32[2048,128]{1,0:T(8,128)} %bitcast.25, bf16[8,256,256]{2,1,0:T(8,128)(2,1)} %get-tuple-element.37.refs_1_, bf16[8,256,256]{2,1,0:T(8,128)(2,1)} %get-tuple-element.38.refs_2_, ...), custom_call_target="tpu_custom_call" | custom-call | flops 1000 | bytes 1000 | tf_op jit(solution)/shard_map/attend/pallas_call | solution.py:254
  82.8 0.0 all-to-all-done.3
  82.8 7.2 %all-to-all-start.4 = ((bf16[8,8,56,128]{3,2,1,0:T(8,128)(2,1)}), bf16[8,8,56,128]{3,2,1,0:T(8,128)(2,1)S(1)}, u32[]{:S(2)}, u32[]{:S(2)}) async-start(bf16[8,8,56,128]{3,2,1,0:T(8,128)(2,1)} %bitcast.29), calls=%async_computation.4 | async-start | bytes 1835008 | tf_op jit(solution)/shard_map/all_to_all | solution.py:426
  90.0 0.1 reduce_sum.36
  90.1 12.2 %all-to-all-done.4 = bf16[8,8,56,128]{3,2,1,0:T(8,128)(2,1)S(1)} async-done(((bf16[8,8,56,128]{3,2,1,0:T(8,128)(2,1)}), bf16[8,8,56,128]{3,2,1,0:T(8,128)(2,1)S(1)}, u32[]{:S(2)}, u32[]{:S(2)}) %all-to-all-start.4) | async-done | bytes 917536 | tf_op jit(solution)/shard_map/all_to_all | solution.py:426
  102.4 0.1 reduce_sum.37
  102.5 0.7 pad_maximum_fusion
  103.2 4.2 %all-to-all-start.5 = ((bf16[8,104,128]{2,1,0:T(8,128)(2,1)}), bf16[8,104,128]{2,1,0:T(8,128)(2,1)S(1)}, u32[]{:S(2)}, u32[]{:S(2)}) async-start(bf16[8,104,128]{2,1,0:T(8,128)(2,1)} %pad_maximum_fusion), calls=%async_computation.5 | async-start | bytes 425984 | tf_op jit(solution)/shard_map/all_to_all | solution.py:426
  107.4 8.3 %inputs_grad.1 = (bf16[8,256,256]{2,1,0:T(8,128)(2,1)}, f32[8,128]{1,0:T(8,128)}) custom-call(bf16[8,256,256]{2,1,0:T(8,128)(2,1)} %bitcast.24, bf16[256,1024]{1,0:T(8,128)(2,1)} %refs_1_.1, f32[1,256]{1,0:T(1,128)} %bitcast.35, bf16[8,4,128,256]{3,2,1,0:T(8,128)(2,1)} %get-tuple-element.46.refs_3_, bf16[8,4,128,256]{3,2,1,0:T(8,128)(2,1)} %get-tuple-element.49.refs_4_, ...), custom_call_target="tpu_custom_call" | custom-call | flops 1000 | bytes 1000 | tf_op jit(solution)/shard_map/inputs_grad/pallas_call | solution.py:307
  115.7 1.7 %all-to-all-done.5.parts_ref = bf16[8,104,128]{2,1,0:T(8,128)(2,1)S(1)} async-done(((bf16[8,104,128]{2,1,0:T(8,128)(2,1)}), bf16[8,104,128]{2,1,0:T(8,128)(2,1)S(1)}, u32[]{:S(2)}, u32[]{:S(2)}) %all-to-all-start.5) | async-done | bytes 213024 | tf_op jit(solution)/shard_map/all_to_all | solution.py:426
  117.4 0.0 copy-start.3
  117.4 0.7 copy-done.3
  118.1 3.4 %pair_grad.1 = (bf16[4,256,128]{2,1,0:T(8,128)(2,1)}, f32[56,128]{1,0:T(8,128)}) custom-call(bf16[8,104,128]{2,1,0:T(8,128)(2,1)} %copy-done.3, f32[8,128]{1,0:T(8,128)} %get-tuple-element.55.small_ref, bf16[4,256,128]{2,1,0:T(8,128)(2,1)} %bitcast.28, f32[1,128]{1,0:T(1,128)} %bitcast.37, bf16[8,128]{1,0:T(8,128)(2,1)} %bitcast.33), custom_call_target="tpu_custom_call" | custom-call | flops 1000 | bytes 1000 | tf_op jit(solution)/shard_map/pair_grad/pallas_call | solution.py:412
  121.5 0.0 collective-permute-start.2
  121.5 1.4 collective-permute-start.1
  122.9 0.4 collective-permute-start
  123.3 1.9 %collective-permute-done.2 = f32[56,128]{1,0:T(8,128)S(1)} collective-permute-done((f32[56,128]{1,0:T(8,128)}, f32[56,128]{1,0:T(8,128)S(1)}, u32[]{:S(2)}, u32[]{:S(2)}) %collective-permute-start.2) | collective-permute-done | bytes 28704 | tf_op jit(solution)/shard_map/ppermute | solution.py:455
  125.3 0.3 collective-permute-done.1
  125.6 0.0 collective-permute-done
  125.6 0.8 add_convert_fusion
  126.4 14.6 %all_to_all.41 = bf16[8,56,128]{2,1,0:T(8,128)(2,1)S(1)} all-to-all(bf16[8,56,128]{2,1,0:T(8,128)(2,1)S(1)} %broadcast_in_dim.13), channel_id=1, replica_groups=mesh['x_lo'=2,'core'=2,'y'=4,'z'=8,'x_hi'=2] {'z'}, dimensions={0} | all-to-all | bytes 229376 | tf_op jit(solution)/shard_map/all_to_all | solution.py:426
  141.0 0.1 broadcast_in_dim.28
  141.1 15.7 %all_to_all.42.total_ref = bf16[8,336,128]{2,1,0:T(8,128)(2,1)} all-to-all(bf16[8,336,128]{2,1,0:T(8,128)(2,1)S(1)} %broadcast_in_dim.28), channel_id=1, replica_groups=mesh['x_lo'=2,'core'=2,'y'=4,'z'=8,'x_hi'=2] {'y','x_hi'}, dimensions={0} | all-to-all | bytes 1376256 | tf_op jit(solution)/shard_map/all_to_all | solution.py:426
  156.8 2.5 %unpack.1 = (f32[256,1024]{1,0:T(8,128)}, f32[256,256]{1,0:T(8,128)}, f32[1,256]{1,0:T(1,128)}, f32[1,256]{1,0:T(1,128)}, f32[1,256]{1,0:T(1,128)}, /*index=5*/f32[1,128]{1,0:T(1,128)}, f32[8,128]{1,0:T(8,128)}) custom-call(bf16[8,336,128]{2,1,0:T(8,128)(2,1)} %all_to_all.42.total_ref), custom_call_target="tpu_custom_call" | custom-call | flops 1000 | bytes 1000 | tf_op jit(solution)/shard_map/unpack/pallas_call | solution.py:345
  (9 shorter events, 0.1 us)
Async XLA Ops:
  23.2 7.1 %copy-start.2 = (f32[8,64,128]{2,1,0:T(8,128)}, f32[8,64,128]{2,1,0:T(8,128)S(1)}, u32[]{:S(2)}) copy-start(f32[8,64,128]{2,1,0:T(8,128)S(1)} %all_to_all.40.column_ref) | copy-start | bytes 786436
  24.3 21.5 %all-to-all-start.1 = ((f32[8,8,32,128]{3,2,1,0:T(8,128)}), f32[8,8,32,128]{3,2,1,0:T(8,128)S(1)}, u32[]{:S(2)}, u32[]{:S(2)}) async-start(f32[8,8,32,128]{3,2,1,0:T(8,128)} %broadcast_in_dim.10), calls=%async_computation.1 | async-start | bytes 2097152 | tf_op jit(solution)/shard_map/all_to_all | solution.py:426
  45.8 3.6 %copy-start.1 = (f32[8,8,32,128]{3,2,1,0:T(8,128)}, f32[8,8,32,128]{3,2,1,0:T(8,128)S(1)}, u32[]{:S(2)}) copy-start(f32[8,8,32,128]{3,2,1,0:T(8,128)S(1)} %all-to-all-done.1) | copy-start | bytes 3145732
  45.8 18.4 %all-to-all-start.2 = ((f32[8,256,128]{2,1,0:T(8,128)}), f32[8,256,128]{2,1,0:T(8,128)S(1)}, u32[]{:S(2)}, u32[]{:S(2)}) async-start(f32[8,256,128]{2,1,0:T(8,128)} %get-tuple-element.47), calls=%async_computation.2 | async-start | bytes 2097152 | tf_op jit(solution)/shard_map/all_to_all | solution.py:426
  64.2 5.4 %copy-start = (f32[8,256,128]{2,1,0:T(8,128)}, f32[8,256,128]{2,1,0:T(8,128)S(1)}, u32[]{:S(2)}) copy-start(f32[8,256,128]{2,1,0:T(8,128)S(1)} %all-to-all-done.2) | copy-start | bytes 3145732
  64.3 18.5 %all-to-all-start.3 = ((bf16[8,8,48,128]{3,2,1,0:T(8,128)(2,1)}), bf16[8,8,48,128]{3,2,1,0:T(8,128)(2,1)S(1)}, u32[]{:S(2)}, u32[]{:S(2)}) async-start(bf16[8,8,48,128]{3,2,1,0:T(8,128)(2,1)} %bitcast.30), calls=%async_computation.3 | async-start | bytes 1572864 | tf_op jit(solution)/shard_map/all_to_all | solution.py:426
  82.8 19.6 %all-to-all-start.4 = ((bf16[8,8,56,128]{3,2,1,0:T(8,128)(2,1)}), bf16[8,8,56,128]{3,2,1,0:T(8,128)(2,1)S(1)}, u32[]{:S(2)}, u32[]{:S(2)}) async-start(bf16[8,8,56,128]{3,2,1,0:T(8,128)(2,1)} %bitcast.29), calls=%async_computation.4 | async-start | bytes 1835008 | tf_op jit(solution)/shard_map/all_to_all | solution.py:426
  103.2 14.2 %all-to-all-start.5 = ((bf16[8,104,128]{2,1,0:T(8,128)(2,1)}), bf16[8,104,128]{2,1,0:T(8,128)(2,1)S(1)}, u32[]{:S(2)}, u32[]{:S(2)}) async-start(bf16[8,104,128]{2,1,0:T(8,128)(2,1)} %pad_maximum_fusion), calls=%async_computation.5 | async-start | bytes 425984 | tf_op jit(solution)/shard_map/all_to_all | solution.py:426
  117.4 0.7 copy-start.3
  121.5 3.8 %collective-permute-start.2 = (f32[56,128]{1,0:T(8,128)}, f32[56,128]{1,0:T(8,128)S(1)}, u32[]{:S(2)}, u32[]{:S(2)}) collective-permute-start(f32[56,128]{1,0:T(8,128)} %get-tuple-element.57), channel_id=1, source_target_pairs={{0,192},{64,128},{128,64},{192,0},{1,193},{65,129},{129,65},{193,1... | collective-permute-start | bytes 86024 | tf_op jit(solution)/shard_map/ppermute | solution.py:455
  121.5 4.1 %collective-permute-start.1 = (f32[56,128]{1,0:T(8,128)}, f32[56,128]{1,0:T(8,128)S(1)}, u32[]{:S(2)}, u32[]{:S(2)}) collective-permute-start(f32[56,128]{1,0:T(8,128)} %get-tuple-element.57), channel_id=1, source_target_pairs={{0,128},{64,192},{128,0},{192,64},{1,129},{65,193},{129,1},{193,65... | collective-permute-start | bytes 86024 | tf_op jit(solution)/shard_map/ppermute | solution.py:455
  122.9 2.7 %collective-permute-start = (f32[56,128]{1,0:T(8,128)}, f32[56,128]{1,0:T(8,128)S(1)}, u32[]{:S(2)}, u32[]{:S(2)}) collective-permute-start(f32[56,128]{1,0:T(8,128)} %get-tuple-element.57), channel_id=1, source_target_pairs={{0,64},{64,0},{128,192},{192,128},{1,65},{65,1},{129,193},{193,129... | collective-permute-start | bytes 86024 | tf_op jit(solution)/shard_map/ppermute | solution.py:455

commit v4 on v3

--- a/solution.py
+++ b/solution.py
@@ -9,8 +9,36 @@
 F32 = jnp.float32
 BF16 = jnp.bfloat16
 AXIAL = ("y", "z", "x_hi")
-PLANE = ("y", "x_hi")
-SENT = [(y * 2 + x) * 8 + z for y in range(4) for z in range(8) for x in range(2)]
+BIAS_INNER, BIAS_OUTER = ("z",), ("y", "x_hi")
+GRAD_INNER, GRAD_OUTER = ("z", "x_hi"), ("y",)
+BACK_INNER, BACK_OUTER = ("z",), ("y", "x_hi")
+SIZES = {"y": 4, "z": 8, "x_hi": 2}
+
+
+def count(axes):
+    total = 1
+    for axis in axes:
+        total *= SIZES[axis]
+    return total
+
+
+def places(outer, inner):
+    result = []
+    for y in range(4):
+        for z in range(8):
+            for x in range(2):
+                place = 0
+                for axis in outer + inner:
+                    place = place * SIZES[axis] + {"y": y, "z": z, "x_hi": x}[axis]
+                result.append(place)
+    return result
+
+
+BIAS_SENT = places(BIAS_OUTER, BIAS_INNER)
+GRAD_SENT = places(GRAD_OUTER, GRAD_INNER)
+BACK_SENT = places(BACK_OUTER, BACK_INNER)
+BI, BO, GI, GO = (count(axes) for axes in (BIAS_INNER, BIAS_OUTER, GRAD_INNER, GRAD_OUTER))
+RI, RO = count(BACK_INNER), count(BACK_OUTER)
 TINY = pl.CostEstimate(flops=1000, bytes_accessed=1000, transcendentals=0)
 FIRST = [(side, 8 * n) for side in range(2) for n in range(64)]
 SECOND = [(0, side, 8 * n) for side in range(2) for n in range(64, 80)]
@@ -25,7 +53,7 @@
     [packed_row(0, *g) for g in FIRST[2 * d : 2 * d + 2]] + [packed_row(*g) for g in SECOND[3 * d : 3 * d + 3]]
     for d in range(64)
 ]
-VMEM_LIMIT = 56 * 1024 * 1024
+MIB = 1024 * 1024
 
 NN = (((1,), (0,)), ((), ()))
 NT = (((1,), (1,)), ((), ()))
@@ -50,48 +78,50 @@
     def _():
         wt_ref[...] = w_ref[...].astype(F32).T.astype(BF16)
         gcol_ref[...] = jnp.broadcast_to(gbias_ref[...], (128, 256)).T
-        for r in range(8):
-            for z in range(8):
+        for r in range(BO):
+            for z in range(BI):
                 copies_ref[r, 32 * z : 32 * z + 32, :] = column_ref[z, 32:64, :]
 
-    unit, _ = norm_rows(x_ref[0].astype(F32))
+    unit, _ = norm_rows(x_ref[...].reshape(512, 256).astype(F32))
     xn = (unit * gain_ref[...] + shift_ref[...]).astype(BF16)
-    xn_ref[0] = xn
+    xn_ref[...] = xn.reshape(2, 256, 256)
+    k_ref[...] = mm(xn, w_ref[:, 256:512]).astype(BF16).reshape(2, 256, 256)
+    v_ref[...] = mm(xn, w_ref[:, 512:768]).astype(BF16).reshape(2, 256, 256)
     factor = 32 ** (-0.5)
-    qt_ref[0] = (mm(wt_ref[0:256, :], xn, NT) * factor).astype(BF16)
-    kt_ref[0] = mm(wt_ref[256:512, :], xn, NT).astype(BF16)
-    vt_ref[0] = mm(wt_ref[512:768, :], xn, NT).astype(BF16)
-    k_ref[0] = mm(xn, w_ref[:, 256:512]).astype(BF16)
-    v_ref[0] = mm(xn, w_ref[:, 512:768]).astype(BF16)
     shifted = jnp.concatenate([gcol_ref[...], gcol_ref[...]], axis=1)
-    gate = jax.nn.sigmoid(mm(wt_ref[768:1024, :], xn, NT) + shifted)
-    dgated = mm(wo_ref[...], adj_ref[0], NT)
-    gt_ref[0] = gate
-    dgt_ref[0] = dgated
-    dat_ref[0] = (dgated * gate).astype(BF16)
+    for r in range(2):
+        row = xn[256 * r : 256 * r + 256]
+        qt_ref[r] = (mm(wt_ref[0:256, :], row, NT) * factor).astype(BF16)
+        kt_ref[r] = mm(wt_ref[256:512, :], row, NT).astype(BF16)
+        vt_ref[r] = mm(wt_ref[512:768, :], row, NT).astype(BF16)
+        gate = jax.nn.sigmoid(mm(wt_ref[768:1024, :], row, NT) + shifted)
+        dgated = mm(wo_ref[...], adj_ref[r], NT)
+        gt_ref[r] = gate
+        dgt_ref[r] = dgated
+        dat_ref[r] = (dgated * gate).astype(BF16)
 
 
 def project(x, adj, w, wo, gain, shift, gbias, column):
     rows = x.shape[0]
-    block = pl.BlockSpec((1, 256, 256), lambda s: (s, 0, 0))
+    block = pl.BlockSpec((2, 256, 256), lambda s: (s, 0, 0))
     whole = lambda a: pl.BlockSpec(a.shape, lambda s: (0,) * a.ndim)
     small = jax.ShapeDtypeStruct((rows, 256, 256), BF16)
     big = jax.ShapeDtypeStruct((rows, 256, 256), F32)
     return pl.pallas_call(
         project_kernel,
-        grid=(rows,),
+        grid=(rows // 2,),
         in_specs=[block, block, whole(w), whole(wo), whole(gain), whole(shift), whole(gbias), whole(column)],
-        out_specs=[block] * 9 + [pl.BlockSpec((8, 256, 128), lambda s: (0, 0, 0))],
-        out_shape=[small] * 5 + [big, big, small, small, jax.ShapeDtypeStruct((8, 256, 128), F32)],
+        out_specs=[block] * 9 + [pl.BlockSpec((BO, 32 * BI, 128), lambda s: (0, 0, 0))],
+        out_shape=[small] * 5 + [big, big, small, small, jax.ShapeDtypeStruct((BO, 32 * BI, 128), F32)],
         scratch_shapes=[pltpu.VMEM((1024, 256), BF16), pltpu.VMEM((256, 128), F32)],
-        compiler_params=pltpu.CompilerParams(vmem_limit_bytes=VMEM_LIMIT),
+        compiler_params=pltpu.CompilerParams(vmem_limit_bytes=56 * MIB),
         cost_estimate=TINY,
         name="project",
     )(x, adj, w, wo, gain, shift, gbias, column)
 
 
 def attend_kernel(
-    heads, first, rows, last,
+    heads, rows, last,
     bias_ref, qt_ref, kt_ref, vt_ref, k_ref, v_ref, gt_ref, dgt_ref, dat_ref, xn_ref, adj_ref, *refs
 ):
     if last:
@@ -103,7 +133,7 @@
 
     @pl.when(step == 0)
     def _():
-        for natural, sent in enumerate(SENT):
+        for natural, sent in enumerate(BIAS_SENT):
             out_ref[32 * natural : 32 * natural + 32, :] = bias_ref[32 * sent : 32 * sent + 32, :]
         for h in range(heads):
             for side in range(2):
@@ -125,14 +155,12 @@
     gated = [[] for _ in range(2)]
 
     def place(h):
-        head = first + h
-        return slice(32 * head, 32 * head + 32), head // 4, head % 4
+        return slice(32 * h, 32 * h + 32)
 
     def score(r, h):
-        here, group, at = place(h)
-        lanes = slice(128 * group, 128 * group + 128)
-        st = mm(k_ref[r, :, lanes], own(qt_ref[r, here, :], at))
-        dpt = mm(v_ref[r, :, lanes], own(dat_ref[r, here, :], at))
+        here = place(h)
+        st = mm(k_ref[r], own(qt_ref[r, here, :], h))
+        dpt = mm(v_ref[r], own(dat_ref[r, here, :], h))
         return st, dpt
 
     def soft(r, h, st, dpt):
@@ -160,7 +188,7 @@
         return jnp.concatenate(ps, axis=1), jnp.concatenate(dss, axis=1)
 
     def close(r, h, p_low, ds_low):
-        here, _, _ = place(h)
+        here = place(h)
         out = slice(32 * h, 32 * h + 32)
         att = mm(vt_ref[r, here, :], p_low)
         g = gt_ref[r, here, :]
@@ -196,7 +224,7 @@
             for side in range(2):
                 part = acc_ref[h, 128 * side : 128 * side + 128, :]
                 out_ref[pl.ds(side * heads + h, 256, stride=2 * heads), :] = part.T
-        for natural, sent in enumerate(SENT):
+        for natural, sent in enumerate(GRAD_SENT):
             stage_ref[sent, 0:32, :] = out_ref[32 * natural : 32 * natural + 32, :]
         if not last:
             for n, (side, row) in enumerate(FIRST):
@@ -215,16 +243,19 @@
         send_ref[...] = stage_ref[...].astype(BF16)
 
 
-def attend(bias, qt, kt, vt, k, v, gt, dgt, dat, xn, adj, first, other):
+def attend(bias, qt, kt, vt, k, v, gt, dgt, dat, xn, adj, chunk, other):
     rows, heads = qt.shape[0], 4
     last = other is not None
     block = pl.BlockSpec((2, 256, 256), lambda s: (s, 0, 0))
     width = 32 * heads
 
     def kernel(*refs):
-        attend_kernel(heads, first, rows, last, *refs)
-
-    in_specs = [pl.BlockSpec((512 * heads, 128), lambda s: (0, 0))] + [block] * 10
+        attend_kernel(heads, rows, last, *refs)
+
+    half = pl.BlockSpec((2, width, 256), lambda s: (s, chunk, 0))
+    columns = pl.BlockSpec((2, 256, width), lambda s: (s, 0, chunk))
+    in_specs = [pl.BlockSpec((512 * heads, 128), lambda s: (0, 0))]
+    in_specs += [half, half, half, columns, columns, half, half, half, block, block]
     out_specs = [
         pl.BlockSpec((2, 4, width, 256), lambda s: (s, 0, 0, 0)),
         pl.BlockSpec((width, 128), lambda s: (0, 0)),
@@ -258,15 +289,15 @@
         out_specs=out_specs,
         out_shape=out_shape,
         scratch_shapes=scratch,
-        compiler_params=pltpu.CompilerParams(vmem_limit_bytes=VMEM_LIMIT),
+        compiler_params=pltpu.CompilerParams(vmem_limit_bytes=56 * MIB),
         cost_estimate=TINY,
         name="attend",
     )(*operands)
 
 
 def inputs_kernel(
-    rows, x_ref, w_ref, gain_ref, dpa_ref, dpb_ref, gba_ref, gbb_ref,
-    dx_ref, small_ref, mg_ref, mb_ref,
+    rows, x_ref, w_ref, gain_ref, dpa_ref, dpb_ref, gba_ref, gbb_ref, pair_ref, pgain_ref,
+    dx_ref, small_ref, normed_ref, mg_ref, mb_ref,
 ):
     step = pl.program_id(0)
 
@@ -274,6 +305,12 @@
     def _():
         mg_ref[...] = jnp.zeros_like(mg_ref)
         mb_ref[...] = jnp.zeros_like(mb_ref)
+
+    pair_unit, _ = norm_rows(pair_ref[0].astype(F32))
+    high = pair_unit.astype(BF16)
+    normed_ref[:, 0:128] = (pair_unit * pgain_ref[...]).astype(BF16)
+    normed_ref[:, 128:256] = high
+    normed_ref[:, 256:384] = (pair_unit - high.astype(F32)).astype(BF16)
 
     unit, inverse = norm_rows(x_ref[0].astype(F32))
     gain = gain_ref[...]
@@ -295,7 +332,7 @@
         )
 
 
-def inputs_grad(x, w, gain, dp_a, dp_b, gb_a, gb_b):
+def inputs_grad(x, w, gain, dp_a, dp_b, gb_a, gb_b, pair, pair_gain):
     rows = x.shape[0]
     block = pl.BlockSpec((1, 256, 256), lambda s: (s, 0, 0))
     quad = pl.BlockSpec((1, 4, 128, 256), lambda s: (s, 0, 0, 0))
@@ -307,33 +344,41 @@
     return pl.pallas_call(
         kernel,
         grid=(rows,),
-        in_specs=[block, whole(w), whole(gain), quad, quad, whole(gb_a), whole(gb_b)],
-        out_specs=[block, pl.BlockSpec((8, 128), lambda s: (0, 0))],
+        in_specs=[
+            block, whole(w), whole(gain), quad, quad, whole(gb_a), whole(gb_b),
+            pl.BlockSpec((1, 128, 128), lambda s: (s // 2, s % 2, 0)), whole(pair_gain),
+        ],
+        out_specs=[
+            block,
+            pl.BlockSpec((8, 128), lambda s: (0, 0)),
+            pl.BlockSpec((128, 384), lambda s: (s, 0)),
+        ],
         out_shape=[
             jax.ShapeDtypeStruct((rows, 256, 256), BF16),
             jax.ShapeDtypeStruct((8, 128), F32),
+            jax.ShapeDtypeStruct((1024, 384), BF16),
         ],
         scratch_shapes=[pltpu.VMEM((1, 256), F32), pltpu.VMEM((1, 256), F32)],
-        compiler_params=pltpu.CompilerParams(vmem_limit_bytes=VMEM_LIMIT),
+        compiler_params=pltpu.CompilerParams(vmem_limit_bytes=56 * MIB),
         cost_estimate=TINY,
         name="inputs_grad",
-    )(x, w, gain, dp_a, dp_b, gb_a, gb_b)
+    )(x, w, gain, dp_a, dp_b, gb_a, gb_b, pair, pair_gain)
 
 
 def unpack_kernel(total_ref, dw_ref, dwo_ref, gb_ref, mg_ref, mb_ref, pg_ref, wb_ref, all_ref, main_ref):
     f = float(524288) ** (-0.5)
     fp = float(262144) ** (-0.5)
     all_ref[...] = total_ref[...].astype(F32)
-    for d in range(64):
-        for k, row in enumerate(GROUPS[d]):
-            at = 40 * (d % 8) + 8 * k
-            main_ref[row : row + 8, :] = all_ref[d // 8, at : at + 8, :] * f
+    for sent, back in zip(GRAD_SENT, BACK_SENT):
+        for k, row in enumerate(GROUPS[sent]):
+            at = 40 * (back % RI) + 8 * k
+            main_ref[row : row + 8, :] = all_ref[back // RI, at : at + 8, :] * f
     for side in range(2):
         lanes = slice(128 * side, 128 * side + 128)
         base = 1280 * side
         dw_ref[lanes, :] = main_ref[base : base + 1024, :].T
         dwo_ref[:, lanes] = main_ref[base + 1024 : base + 1280, :]
-    tail = jnp.sum(all_ref[:, 320:336, :], axis=0)
+    tail = jnp.sum(all_ref[:, 40 * RI :, :], axis=0)
     for n, ref in enumerate((gb_ref, mg_ref, mb_ref)):
         ref[...] = jnp.concatenate([tail[2 * n : 2 * n + 1], tail[2 * n + 1 : 2 * n + 2]], axis=1) * f
     pg_ref[...] = tail[6:7] * fp
@@ -351,8 +396,8 @@
             jax.ShapeDtypeStruct((1, 128), F32),
             jax.ShapeDtypeStruct((8, 128), F32),
         ],
-        scratch_shapes=[pltpu.VMEM((8, 336, 128), F32), pltpu.VMEM((2560, 128), F32)],
-        compiler_params=pltpu.CompilerParams(vmem_limit_bytes=VMEM_LIMIT),
+        scratch_shapes=[pltpu.VMEM((RO, 40 * RI + 16, 128), F32), pltpu.VMEM((2560, 128), F32)],
+        compiler_params=pltpu.CompilerParams(vmem_limit_bytes=12 * MIB),
         cost_estimate=TINY,
         name="unpack",
     )(total)
@@ -365,7 +410,7 @@
             unit, _ = norm_rows(pair_ref[i, 128 * side : 128 * side + 128, :].astype(F32))
             both = mm(wt, (unit * gain_ref[...]).astype(BF16), NT)
             at = 8 * i + 4 * side
-            for r in range(8):
+            for r in range(BI):
                 own_ref[r, at : at + 4, :] = both[0:4]
                 own_ref[r, 32 + at : 36 + at, :] = both[4:8]
 
@@ -373,19 +418,47 @@
 def pair_bias(pair, gain, wt):
     return pl.pallas_call(
         pair_bias_kernel,
-        out_shape=jax.ShapeDtypeStruct((8, 64, 128), F32),
-        compiler_params=pltpu.CompilerParams(vmem_limit_bytes=VMEM_LIMIT),
+        out_shape=jax.ShapeDtypeStruct((BI, 64, 128), F32),
+        compiler_params=pltpu.CompilerParams(vmem_limit_bytes=56 * MIB),
         cost_estimate=TINY,
         name="pair_bias",
     )(pair, gain, wt)
 
 
-def pair_grad_kernel(parts_ref, small_ref, pair_ref, gain_ref, wt_ref, dpair_ref, block_ref, mine_ref):
-    mine_ref[...] = jnp.sum(parts_ref[...].astype(F32), axis=0)
+def pair_sums_kernel(parts_ref, small_ref, normed_ref, wt_ref, block_ref, mine_ref):
+    mine = jnp.sum(parts_ref[...].astype(F32), axis=0)
+    mine_ref[...] = mine[0:64]
+    tiles = []
+    for tile in range(8):
+        at = 4 * tile
+        tiles.append(jnp.concatenate([mine[at : at + 4], mine[32 + at : 36 + at]], axis=0))
+    d_bias = jnp.concatenate(tiles, axis=1)
+    high = d_bias.astype(BF16).astype(F32)
+    pieces = jnp.concatenate([high, d_bias - high], axis=0).astype(BF16)
+    both = mm(pieces, normed_ref[...])
+    both = both[0:8] + both[8:16]
+    d_pg = jnp.sum((both[:, 128:256] + both[:, 256:384]) * wt_ref[...].astype(F32), axis=0, keepdims=True)
+    block_ref[0:40, :] = mine[64:104]
+    block_ref[40:48, :] = jnp.concatenate([small_ref[0:6, :], d_pg, small_ref[7:8, :]], axis=0)
+    block_ref[48:56, :] = both[:, 0:128]
+
+
+def pair_sums(parts, small, normed, wt):
+    return pl.pallas_call(
+        pair_sums_kernel,
+        out_shape=[
+            jax.ShapeDtypeStruct((56, 128), F32),
+            jax.ShapeDtypeStruct((64, 128), F32),
+        ],
+        compiler_params=pltpu.CompilerParams(vmem_limit_bytes=8 * MIB),
+        cost_estimate=TINY,
+        name="pair_sums",
+    )(parts, small, normed, wt)
+
+
+def pair_grad_kernel(mine_ref, pair_ref, gain_ref, wt_ref, dpair_ref):
     wt = jnp.concatenate([wt_ref[...].astype(F32)] * 2, axis=0).astype(BF16)
     gain = gain_ref[...]
-    d_wb = jnp.zeros((8, 128), F32)
-    d_pg = jnp.zeros((1, 128), F32)
     for i in range(4):
         for side in range(2):
             here = slice(128 * side, 128 * side + 128)
@@ -394,32 +467,20 @@
             high = d_bias.astype(BF16).astype(F32)
             pieces = jnp.concatenate([high, d_bias - high], axis=0)
             unit, inverse = norm_rows(pair_ref[i, here, :].astype(F32))
-            normed = (unit * gain).astype(BF16)
-            dpn = mm(pieces.T.astype(BF16), wt)
-            both = mm(pieces.astype(BF16), normed)
-            d_wb += both[0:8] + both[8:16]
-            d_pg += jnp.sum(unit * dpn, axis=0, keepdims=True)
-            g = dpn * gain
+            g = mm(pieces.T.astype(BF16), wt) * gain
             mean = jnp.mean(g, axis=-1, keepdims=True)
             cross = jnp.mean(g * unit, axis=-1, keepdims=True)
             dpair_ref[i, here, :] = (inverse * (g - mean - unit * cross)).astype(BF16)
-    block_ref[0:40, :] = mine_ref[64:104, :]
-    block_ref[40:48, :] = jnp.concatenate([small_ref[0:6, :], d_pg, small_ref[7:8, :]], axis=0)
-    block_ref[48:56, :] = d_wb
-
-
-def pair_grad(parts, small, pair, gain, wt):
+
+
+def pair_grad(mine, pair, gain, wt):
     return pl.pallas_call(
         pair_grad_kernel,
-        out_shape=[
-            jax.ShapeDtypeStruct((4, 256, 128), BF16),
-            jax.ShapeDtypeStruct((56, 128), F32),
-        ],
-        scratch_shapes=[pltpu.VMEM((104, 128), F32)],
-        compiler_params=pltpu.CompilerParams(vmem_limit_bytes=VMEM_LIMIT),
+        out_shape=jax.ShapeDtypeStruct((4, 256, 128), BF16),
+        compiler_params=pltpu.CompilerParams(vmem_limit_bytes=8 * MIB),
         cost_estimate=TINY,
         name="pair_grad",
-    )(parts, small, pair, gain, wt)
+    )(mine, pair, gain, wt)
 
 
 def exchange(blocks, axes):
@@ -435,29 +496,28 @@
     gain2, shift2 = gain.reshape(1, 256), shift.reshape(1, 256)
     pair_gain2 = pair_gain.reshape(1, 128)
     pair_wt = pair_w.T
-    column = exchange(pair_bias(pair, pair_gain2, pair_wt), "z")
-    bias_a = spread(column[:, :32], 8, PLANE).reshape(2048, 128)
+    column = exchange(pair_bias(pair, pair_gain2, pair_wt), BIAS_INNER)
+    bias_a = spread(column[:, :32], BO, BIAS_OUTER).reshape(2048, 128)
     *made, copies = project(x, adj, w, wo, gain2, shift2, gbias.reshape(1, 256), column)
-    bias_b = exchange(copies, PLANE).reshape(2048, 128)
+    bias_b = exchange(copies, BIAS_OUTER).reshape(2048, 128)
 
     dp_a, gb_a, send_a, grad_a = attend(bias_a, *made, adj, 0, None)
-    dp_b, gb_b, send_b = attend(bias_b, *made, adj, 4, grad_a)
-    dx, small = inputs_grad(x, w, gain2, dp_a, dp_b, gb_a, gb_b)
-
-    sums = [
-        jnp.sum(exchange(t.reshape(8, 8, -1, 128), PLANE).astype(F32), axis=0).astype(BF16)
-        for t in (send_a, send_b)
-    ]
-    order = [sums[0][:, :32], sums[1][:, :32], sums[0][:, 32:], sums[1][:, 32:]]
-    parts = exchange(jnp.concatenate(order, axis=1), "z")
-    dpair, block = pair_grad(parts, small, pair, pair_gain2, pair_wt)
+    dp_b, gb_b, send_b = attend(bias_b, *made, adj, 1, grad_a)
+    dx, small, normed = inputs_grad(x, w, gain2, dp_a, dp_b, gb_a, gb_b, pair, pair_gain2)
+
+    first, second = (exchange(t.reshape(GO, GI, -1, 128), GRAD_OUTER) for t in (send_a, send_b))
+    first, second = (jnp.sum(t.astype(F32), axis=0).astype(BF16) for t in (first, second))
+    order = [first[:, :32], second[:, :32], first[:, 32:], second[:, 32:]]
+    parts = exchange(jnp.concatenate(order, axis=1), GRAD_INNER)
+    block, mine = pair_sums(parts, small, normed, pair_wt)
+    dpair = pair_grad(mine, pair, pair_gain2, pair_wt)
     others = [
         lax.ppermute(block, ("x_lo", "core"), [(n, n ^ flip) for n in range(4)]) for flip in (1, 2, 3)
     ]
     block = (block + others[0]) + (others[1] + others[2])
-    line = spread(block.astype(BF16), 8, "z")
+    line = spread(block.astype(BF16), RI, BACK_INNER)
     tail = jnp.sum(line[:, 40:].astype(F32), axis=0).astype(BF16)
-    total = spread(jnp.concatenate([line[:, :40].reshape(320, 128), tail], axis=0), 8, PLANE)
+    total = spread(jnp.concatenate([line[:, :40].reshape(40 * RI, 128), tail], axis=0), RO, BACK_OUTER)
     dw, dwo, gb, mg, mb, pg, wb = unpack(total)
     return (
         dx[None],

time: 160 us -> 153 us (0.956)
  blocking collectives: 50.6 us -> 32.2 us
  waiting for transfers between devices: 23 us -> 37 us
  Pallas kernels: 52.9 us -> 47.9 us
  local copies, waits for them, and re-layouts: 1.94 us -> 3.95 us
    all_to_all x3 -> x2, blocking collectives: 50.6 us -> 32.2 us  [exchange(): return lax.all_to_all(blocks, axes, 0, 0, tiled=True)]
    all_to_all x5 -> x6, waiting for transfers between devices: 20.8 us -> 34.8 us  [exchange(): return lax.all_to_all(blocks, axes, 0, 0, tiled=True)]
    pallas_call x3 -> x4, Pallas kernels: 16 us -> 13.2 us  [the longest x1 8.13 us: project(): pl.pallas_call(project_kernel, grid=(rows // 2,), in_specs=[block, block,...]
    all_to_all x5 -> x6, starting transfers between devices: 26.4 us -> 27.4 us  [exchange(): return lax.all_to_all(blocks, axes, 0, 0, tiled=True)]
  transfers between devices with their start and end apart: 8 -> 9, of which waited for: 6 -> 7; matrix products, arithmetic and copies ran while one was open for 0% -> 0% of each run, Pallas kernels for 28% -> 29%
where the time goes in v4:
time: 153 us; the launch traced here: 152 us
  Pallas kernels  47.9 us (31%)
  waiting for transfers between devices  37 us (24%)
  blocking collectives  32.2 us (21%)
  starting transfers between devices  29.4 us (19%)
  local copies, waits for them, and re-layouts  3.95 us (3%)
    all_to_all x6, waiting for transfers between devices, exchange(): return lax.all_to_all(blocks, axes, 0, 0, tiled=True)  34.8 us
    all_to_all x2, blocking collectives, exchange(): return lax.all_to_all(blocks, axes, 0, 0, tiled=True)  32.2 us
    all_to_all x6, starting transfers between devices, exchange(): return lax.all_to_all(blocks, axes, 0, 0, tiled=True)  27.4 us
    pallas_call x2, Pallas kernels, attend(): pl.pallas_call(kernel, grid=(rows // 2,), in_specs=in_specs, out_specs=ou...  24.8 us
    pallas_call x1, Pallas kernels, inputs_grad(): pl.pallas_call(kernel, grid=(rows,), in_specs=[block, whole(w), whole(gai...  8.56 us
    pallas_call x1, Pallas kernels, project(): pl.pallas_call(project_kernel, grid=(rows // 2,), in_specs=[block, block,...  8.13 us
  transfers between devices with their start and end apart: 9, of which 7 were waited for; matrix products, arithmetic and copies ran while one was open for 0% of the time, Pallas kernels for 29%

profile of v4, /device:TPU:2, one launch (start us, length us, event | category | flops | bytes accessed | tf_op | source)
XLA Modules:
  0.0 152.2 jit_solution(9719478161957361633)
XLA Ops:
  0.6 2.2 %pair_bias.1 = f32[8,64,128]{2,1,0:T(8,128)} custom-call(bf16[4,256,128]{2,1,0:T(8,128)(2,1)} %bitcast.20, f32[1,128]{1,0:T(1,128)} %bitcast.26, bf16[8,128]{1,0:T(8,128)(2,1)} %bitcast.23), custom_call_target="tpu_custom_call" | custom-call | flops 1000 | bytes 1000 | tf_op jit(solution)/shard_map/pair_bias/pallas_call | solution.py:419
  2.9 20.3 %all_to_all.40.column_ref = f32[8,64,128]{2,1,0:T(8,128)S(1)} all-to-all(f32[8,64,128]{2,1,0:T(8,128)} %pair_bias.1), channel_id=1, replica_groups=mesh['x_lo'=2,'core'=2,'y'=4,'z'=8,'x_hi'=2] {'z'}, dimensions={0} | all-to-all | bytes 524288 | tf_op jit(solution)/shard_map/all_to_all | solution.py:487
  23.2 0.0 copy-start.7
  23.2 1.1 broadcast_in_dim.10
  24.3 6.0 %all-to-all-start.1 = ((f32[8,8,32,128]{3,2,1,0:T(8,128)}), f32[8,8,32,128]{3,2,1,0:T(8,128)S(1)}, u32[]{:S(2)}, u32[]{:S(2)}) async-start(f32[8,8,32,128]{3,2,1,0:T(8,128)} %broadcast_in_dim.10), calls=%async_computation.1 | async-start | bytes 2097152 | tf_op jit(solution)/shard_map/all_to_all | solution.py:487
  30.3 0.0 copy-done.7
  30.3 8.1 %project.1 = (bf16[8,256,256]{2,1,0:T(8,128)(2,1)}, bf16[8,256,256]{2,1,0:T(8,128)(2,1)}, bf16[8,256,256]{2,1,0:T(8,128)(2,1)}, bf16[8,256,256]{2,1,0:T(8,128)(2...) custom-call(bf16[8,256,256]{2,1,0:T(8,128)(2,1)} %bitcast.32, ...), custom_call_target="tpu_custom_call" | custom-call | flops 1000 | bytes 1000 | tf_op jit(solution)/shard_map/project/pallas_call | solution.py:110
  38.5 7.3 %all-to-all-done.1 = f32[8,8,32,128]{3,2,1,0:T(8,128)S(1)} async-done(((f32[8,8,32,128]{3,2,1,0:T(8,128)}), f32[8,8,32,128]{3,2,1,0:T(8,128)S(1)}, u32[]{:S(2)}, u32[]{:S(2)}) %all-to-all-start.1) | async-done | bytes 1048608 | tf_op jit(solution)/shard_map/all_to_all | solution.py:487
  45.8 0.0 copy-start.6
  45.8 3.6 %all-to-all-start.2 = ((f32[8,256,128]{2,1,0:T(8,128)}), f32[8,256,128]{2,1,0:T(8,128)S(1)}, u32[]{:S(2)}, u32[]{:S(2)}) async-start(f32[8,256,128]{2,1,0:T(8,128)} %get-tuple-element.48), calls=%async_computation.2 | async-start | bytes 2097152 | tf_op jit(solution)/shard_map/all_to_all | solution.py:487
  49.4 0.0 copy-done.6
  49.4 12.4 %attend.2 = (bf16[8,4,128,256]{3,2,1,0:T(8,128)(2,1)}, f32[128,128]{1,0:T(8,128)}, bf16[64,48,128]{2,1,0:T(8,128)(2,1)}, f32[2,128,128]{2,1,0:T(8,128)}) custom-call(f32[2048,128]{1,0:T(8,128)} %bitcast.35, bf16[8,256,256]{2,1,0:T(8,128)(2,1)} %get-tuple-element.38.refs_1_, bf16[8,256,256]{2,1,0:T(8,128)(2,1)} %get-tuple-element.39.refs_2_, ...), custom_call_target="tpu_custom_call" | custom-call | flops 1000 | bytes 1000 | tf_op jit(solution)/shard_map/attend/pallas_call | solution.py:285
  61.8 2.5 %all-to-all-done.2 = f32[8,256,128]{2,1,0:T(8,128)S(1)} async-done(((f32[8,256,128]{2,1,0:T(8,128)}), f32[8,256,128]{2,1,0:T(8,128)S(1)}, u32[]{:S(2)}, u32[]{:S(2)}) %all-to-all-start.2) | async-done | bytes 1048608 | tf_op jit(solution)/shard_map/all_to_all | solution.py:487
  64.2 0.0 copy-start.5
  64.3 3.5 %all-to-all-start.3 = ((bf16[4,16,48,128]{3,2,1,0:T(8,128)(2,1)}), bf16[4,16,48,128]{3,2,1,0:T(8,128)(2,1)S(1)}, u32[]{:S(2)}, u32[]{:S(2)}) async-start(bf16[4,16,48,128]{3,2,1,0:T(8,128)(2,1)} %bitcast.37), calls=%async_computation.3 | async-start | bytes 1572864 | tf_op jit(solution)/shard_map/all_to_all | solution.py:487
  67.8 0.0 copy-done.5
  67.8 12.4 %attend.3 = (bf16[8,4,128,256]{3,2,1,0:T(8,128)(2,1)}, f32[128,128]{1,0:T(8,128)}, bf16[64,56,128]{2,1,0:T(8,128)(2,1)}) custom-call(f32[2048,128]{1,0:T(8,128)} %bitcast.34, bf16[8,256,256]{2,1,0:T(8,128)(2,1)} %get-tuple-element.38.refs_1_, bf16[8,256,256]{2,1,0:T(8,128)(2,1)} %get-tuple-element.39.refs_2_, ...), custom_call_target="tpu_custom_call" | custom-call | flops 1000 | bytes 1000 | tf_op jit(solution)/shard_map/attend/pallas_call | solution.py:285
  80.2 0.0 all-to-all-done.3
  80.2 4.7 %all-to-all-start.4 = ((bf16[4,16,56,128]{3,2,1,0:T(8,128)(2,1)}), bf16[4,16,56,128]{3,2,1,0:T(8,128)(2,1)S(1)}, u32[]{:S(2)}, u32[]{:S(2)}) async-start(bf16[4,16,56,128]{3,2,1,0:T(8,128)(2,1)} %bitcast.36), calls=%async_computation.4 | async-start | bytes 1835008 | tf_op jit(solution)/shard_map/all_to_all | solution.py:487
  85.0 0.1 reduce_sum.36
  85.1 10.0 %all-to-all-done.4 = bf16[4,16,56,128]{3,2,1,0:T(8,128)(2,1)S(1)} async-done(((bf16[4,16,56,128]{3,2,1,0:T(8,128)(2,1)}), bf16[4,16,56,128]{3,2,1,0:T(8,128)(2,1)S(1)}, u32[]{:S(2)}, u32[]{:S(2)}) %all-to-all-start.4) | async-done | bytes 917536 | tf_op jit(solution)/shard_map/all_to_all | solution.py:487
  95.1 0.1 reduce_sum.37
  95.3 0.8 pad_maximum_fusion
  96.1 5.6 %all-to-all-start.5 = ((bf16[16,104,128]{2,1,0:T(8,128)(2,1)}), bf16[16,104,128]{2,1,0:T(8,128)(2,1)S(1)}, u32[]{:S(2)}, u32[]{:S(2)}) async-start(bf16[16,104,128]{2,1,0:T(8,128)(2,1)} %pad_maximum_fusion), calls=%async_computation.5 | async-start | bytes 851968 | tf_op jit(solution)/shard_map/all_to_all | solution.py:487
  101.8 0.0 copy-start.2
  101.8 8.6 %inputs_grad.1 = (bf16[8,256,256]{2,1,0:T(8,128)(2,1)}, f32[8,128]{1,0:T(8,128)}, bf16[1024,384]{1,0:T(8,128)(2,1)}) custom-call(bf16[8,256,256]{2,1,0:T(8,128)(2,1)} %bitcast.33, bf16[256,1024]{1,0:T(8,128)(2,1)} %refs_1_.1, f32[1,256]{1,0:T(1,128)} %bitcast.41, bf16[8,4,128,256]{3,2,1,0:T(8,128)(2,1)} %get-tuple-element.47.refs_3_, ...), custom_call_target="tpu_custom_call" | custom-call | flops 1000 | bytes 1000 | tf_op jit(solution)/shard_map/inputs_grad/pallas_call | solution.py:344
  110.3 5.2 %all-to-all-done.5.parts_ref = bf16[16,104,128]{2,1,0:T(8,128)(2,1)S(1)} async-done(((bf16[16,104,128]{2,1,0:T(8,128)(2,1)}), bf16[16,104,128]{2,1,0:T(8,128)(2,1)S(1)}, u32[]{:S(2)}, u32[]{:S(2)}) %all-to-all-start.5) | async-done | bytes 426016 | tf_op jit(solution)/shard_map/all_to_all | solution.py:487
  115.5 0.0 copy-done.2
  115.5 0.0 copy-start.1
  115.5 1.1 copy-done.1
  116.7 0.0 copy-start.4
  116.7 0.7 copy-done.4
  117.3 0.0 copy-start
  117.3 0.0 copy-start.3
  117.3 0.3 pair_sums.1
  117.6 0.1 collective-permute-start.2
  117.7 1.5 collective-permute-start.1
  119.2 0.3 collective-permute-start
  119.6 1.7 %collective-permute-done.2 = f32[56,128]{1,0:T(8,128)S(1)} collective-permute-done((f32[56,128]{1,0:T(8,128)S(1)}, f32[56,128]{1,0:T(8,128)S(1)}, u32[]{:S(2)}, u32[]{:S(2)}) %collective-permute-start.2) | collective-permute-done | bytes 28704 | tf_op jit(solution)/shard_map/ppermute | solution.py:515
  121.3 0.4 collective-permute-done.1
  121.7 0.0 collective-permute-done
  121.7 11.8 %all_to_all.41 = bf16[8,56,128]{2,1,0:T(8,128)(2,1)S(1)} all-to-all(bf16[8,56,128]{2,1,0:T(8,128)(2,1)S(1)} %broadcast_in_dim.13), channel_id=1, replica_groups=mesh['x_lo'=2,'core'=2,'y'=4,'z'=8,'x_hi'=2] {'z'}, dimensions={0} | all-to-all | bytes 229376 | tf_op jit(solution)/shard_map/all_to_all | solution.py:487
  133.6 0.9 broadcast_in_dim.28
  134.5 3.9 %all-to-all-start.7 = ((bf16[8,336,128]{2,1,0:T(8,128)(2,1)}), bf16[8,336,128]{2,1,0:T(8,128)(2,1)S(1)}, u32[]{:S(2)}, u32[]{:S(2)}) async-start(bf16[8,336,128]{2,1,0:T(8,128)(2,1)} %broadcast_in_dim.28), calls=%async_computation.7 | async-start | bytes 1376256 | tf_op jit(solution)/shard_map/all_to_all | solution.py:487
  138.5 0.0 copy-done
  138.5 0.0 copy-done.3
  138.5 2.6 %pair_grad.1 = bf16[4,256,128]{2,1,0:T(8,128)(2,1)} custom-call(f32[64,128]{1,0:T(8,128)S(1)} %get-tuple-element.58.mine_ref, bf16[4,256,128]{2,1,0:T(8,128)(2,1)S(1)} %bitcast.22, f32[1,128]{1,0:T(1,128)S(1)} %bitcast.28, bf16[8,128]{1,0:T(8,128)(2,1)S(1)} %bitcast.25), custom_call_target="tpu_custom_call" | custom-call | flops 1000 | bytes 1000 | tf_op jit(solution)/shard_map/pair_grad/pallas_call | solution.py:477
  141.0 9.8 %all-to-all-done.7.total_ref = bf16[8,336,128]{2,1,0:T(8,128)(2,1)S(1)} async-done(((bf16[8,336,128]{2,1,0:T(8,128)(2,1)}), bf16[8,336,128]{2,1,0:T(8,128)(2,1)S(1)}, u32[]{:S(2)}, u32[]{:S(2)}) %all-to-all-start.7) | async-done | bytes 688160 | tf_op jit(solution)/shard_map/all_to_all | solution.py:487
  150.9 1.4 unpack.1
  (10 shorter events, 0.1 us)
Async XLA Ops:
  23.2 7.1 %copy-start.7 = (f32[8,64,128]{2,1,0:T(8,128)}, f32[8,64,128]{2,1,0:T(8,128)S(1)}, u32[]{:S(2)}) copy-start(f32[8,64,128]{2,1,0:T(8,128)S(1)} %all_to_all.40.column_ref) | copy-start | bytes 786436
  24.3 21.5 %all-to-all-start.1 = ((f32[8,8,32,128]{3,2,1,0:T(8,128)}), f32[8,8,32,128]{3,2,1,0:T(8,128)S(1)}, u32[]{:S(2)}, u32[]{:S(2)}) async-start(f32[8,8,32,128]{3,2,1,0:T(8,128)} %broadcast_in_dim.10), calls=%async_computation.1 | async-start | bytes 2097152 | tf_op jit(solution)/shard_map/all_to_all | solution.py:487
  45.8 3.6 %copy-start.6 = (f32[8,8,32,128]{3,2,1,0:T(8,128)}, f32[8,8,32,128]{3,2,1,0:T(8,128)S(1)}, u32[]{:S(2)}) copy-start(f32[8,8,32,128]{3,2,1,0:T(8,128)S(1)} %all-to-all-done.1) | copy-start | bytes 3145732
  45.8 18.4 %all-to-all-start.2 = ((f32[8,256,128]{2,1,0:T(8,128)}), f32[8,256,128]{2,1,0:T(8,128)S(1)}, u32[]{:S(2)}, u32[]{:S(2)}) async-start(f32[8,256,128]{2,1,0:T(8,128)} %get-tuple-element.48), calls=%async_computation.2 | async-start | bytes 2097152 | tf_op jit(solution)/shard_map/all_to_all | solution.py:487
  64.2 3.5 %copy-start.5 = (f32[8,256,128]{2,1,0:T(8,128)}, f32[8,256,128]{2,1,0:T(8,128)S(1)}, u32[]{:S(2)}) copy-start(f32[8,256,128]{2,1,0:T(8,128)S(1)} %all-to-all-done.2) | copy-start | bytes 3145732
  64.3 15.9 %all-to-all-start.3 = ((bf16[4,16,48,128]{3,2,1,0:T(8,128)(2,1)}), bf16[4,16,48,128]{3,2,1,0:T(8,128)(2,1)S(1)}, u32[]{:S(2)}, u32[]{:S(2)}) async-start(bf16[4,16,48,128]{3,2,1,0:T(8,128)(2,1)} %bitcast.37), calls=%async_computation.3 | async-start | bytes 1572864 | tf_op jit(solution)/shard_map/all_to_all | solution.py:487
  80.2 14.9 %all-to-all-start.4 = ((bf16[4,16,56,128]{3,2,1,0:T(8,128)(2,1)}), bf16[4,16,56,128]{3,2,1,0:T(8,128)(2,1)S(1)}, u32[]{:S(2)}, u32[]{:S(2)}) async-start(bf16[4,16,56,128]{3,2,1,0:T(8,128)(2,1)} %bitcast.36), calls=%async_computation.4 | async-start | bytes 1835008 | tf_op jit(solution)/shard_map/all_to_all | solution.py:487
  96.1 19.4 %all-to-all-start.5 = ((bf16[16,104,128]{2,1,0:T(8,128)(2,1)}), bf16[16,104,128]{2,1,0:T(8,128)(2,1)S(1)}, u32[]{:S(2)}, u32[]{:S(2)}) async-start(bf16[16,104,128]{2,1,0:T(8,128)(2,1)} %pad_maximum_fusion), calls=%async_computation.5 | async-start | bytes 851968 | tf_op jit(solution)/shard_map/all_to_all | solution.py:487
  101.8 13.7 %copy-start.2 = (bf16[128,8]{0,1:T(8,128)(2,1)S(1)}, bf16[128,8]{0,1:T(8,128)(2,1)}, u32[]{:S(2)}) copy-start(bf16[128,8]{0,1:T(8,128)(2,1)} %param.19) | copy-start | bytes 6148
  115.5 1.1 copy-start.1
  116.7 0.7 copy-start.4
  117.3 21.1 %copy-start = (bf16[1,4,256,128]{3,2,1,0:T(8,128)(2,1)S(1)}, bf16[1,4,256,128]{3,2,1,0:T(8,128)(2,1)}, u32[]{:S(2)}) copy-start(bf16[1,4,256,128]{3,2,1,0:T(8,128)(2,1)} %param.11) | copy-start | bytes 786436
  117.3 21.1 %copy-start.3 = (f32[128]{0:T(128)S(1)}, f32[128]{0:T(128)}, u32[]{:S(2)}) copy-start(f32[128]{0:T(128)} %param.18) | copy-start | bytes 1540
  117.6 3.7 %collective-permute-start.2 = (f32[56,128]{1,0:T(8,128)S(1)}, f32[56,128]{1,0:T(8,128)S(1)}, u32[]{:S(2)}, u32[]{:S(2)}) collective-permute-start(f32[56,128]{1,0:T(8,128)S(1)} %get-tuple-element.59), channel_id=1, source_target_pairs={{0,192},{64,128},{128,64},{192,0},{1,193},{65,129},{129,65},{193,1... | collective-permute-start | bytes 86024 | tf_op jit(solution)/shard_map/ppermute | solution.py:515
  117.7 4.0 %collective-permute-start.1 = (f32[56,128]{1,0:T(8,128)S(1)}, f32[56,128]{1,0:T(8,128)S(1)}, u32[]{:S(2)}, u32[]{:S(2)}) collective-permute-start(f32[56,128]{1,0:T(8,128)S(1)} %get-tuple-element.59), channel_id=1, source_target_pairs={{0,128},{64,192},{128,0},{192,64},{1,129},{65,193},{129,1},{193,65... | collective-permute-start | bytes 86024 | tf_op jit(solution)/shard_map/ppermute | solution.py:515
  119.2 2.4 %collective-permute-start = (f32[56,128]{1,0:T(8,128)S(1)}, f32[56,128]{1,0:T(8,128)S(1)}, u32[]{:S(2)}, u32[]{:S(2)}) collective-permute-start(f32[56,128]{1,0:T(8,128)S(1)} %get-tuple-element.59), channel_id=1, source_target_pairs={{0,64},{64,0},{128,192},{192,128},{1,65},{65,1},{129,193},{193,129... | collective-permute-start | bytes 86024 | tf_op jit(solution)/shard_map/ppermute | solution.py:515
  134.5 16.4 %all-to-all-start.7 = ((bf16[8,336,128]{2,1,0:T(8,128)(2,1)}), bf16[8,336,128]{2,1,0:T(8,128)(2,1)S(1)}, u32[]{:S(2)}, u32[]{:S(2)}) async-start(bf16[8,336,128]{2,1,0:T(8,128)(2,1)} %broadcast_in_dim.28), calls=%async_computation.7 | async-start | bytes 1376256 | tf_op jit(solution)/shard_map/all_to_all | solution.py:487

commit v5 on v4

--- a/solution.py
+++ b/solution.py
@@ -72,7 +72,7 @@
 
 def project_kernel(
     x_ref, adj_ref, w_ref, wo_ref, gain_ref, shift_ref, gbias_ref, column_ref,
-    qt_ref, kt_ref, vt_ref, k_ref, v_ref, gt_ref, dgt_ref, dat_ref, xn_ref, copies_ref, wt_ref, gcol_ref,
+    qt_ref, kt_ref, vt_ref, k_ref, v_ref, gt_ref, dat_ref, xn_ref, copies_ref, wt_ref, gcol_ref,
 ):
     @pl.when(pl.program_id(0) == 0)
     def _():
@@ -97,7 +97,6 @@
         gate = jax.nn.sigmoid(mm(wt_ref[768:1024, :], row, NT) + shifted)
         dgated = mm(wo_ref[...], adj_ref[r], NT)
         gt_ref[r] = gate
-        dgt_ref[r] = dgated
         dat_ref[r] = (dgated * gate).astype(BF16)
 
 
@@ -111,8 +110,8 @@
         project_kernel,
         grid=(rows // 2,),
         in_specs=[block, block, whole(w), whole(wo), whole(gain), whole(shift), whole(gbias), whole(column)],
-        out_specs=[block] * 9 + [pl.BlockSpec((BO, 32 * BI, 128), lambda s: (0, 0, 0))],
-        out_shape=[small] * 5 + [big, big, small, small, jax.ShapeDtypeStruct((BO, 32 * BI, 128), F32)],
+        out_specs=[block] * 8 + [pl.BlockSpec((BO, 32 * BI, 128), lambda s: (0, 0, 0))],
+        out_shape=[small] * 5 + [big, small, small, jax.ShapeDtypeStruct((BO, 32 * BI, 128), F32)],
         scratch_shapes=[pltpu.VMEM((1024, 256), BF16), pltpu.VMEM((256, 128), F32)],
         compiler_params=pltpu.CompilerParams(vmem_limit_bytes=56 * MIB),
         cost_estimate=TINY,
@@ -122,7 +121,7 @@
 
 def attend_kernel(
     heads, rows, last,
-    bias_ref, qt_ref, kt_ref, vt_ref, k_ref, v_ref, gt_ref, dgt_ref, dat_ref, xn_ref, adj_ref, *refs
+    bias_ref, qt_ref, kt_ref, vt_ref, k_ref, v_ref, gt_ref, dat_ref, xn_ref, adj_ref, *refs
 ):
     if last:
         other_ref, dp_ref, gb_ref, send_ref, bt_ref, acc_ref, out_ref, w_ref, stage_ref = refs
@@ -192,7 +191,7 @@
         out = slice(32 * h, 32 * h + 32)
         att = mm(vt_ref[r, here, :], p_low)
         g = gt_ref[r, here, :]
-        graw = dgt_ref[r, here, :] * att * g * (1.0 - g)
+        graw = dat_ref[r, here, :].astype(F32) * att * (1.0 - g)
         gated[r].append((g * att).astype(BF16))
         gb_ref[out, :] += graw[:, :128] + graw[:, 128:]
         dp_ref[r, 0, out, :] = (mm(kt_ref[r, here, :], ds_low) * (32 ** (-0.5))).astype(BF16)
@@ -243,7 +242,7 @@
         send_ref[...] = stage_ref[...].astype(BF16)
 
 
-def attend(bias, qt, kt, vt, k, v, gt, dgt, dat, xn, adj, chunk, other):
+def attend(bias, qt, kt, vt, k, v, gt, dat, xn, adj, chunk, other):
     rows, heads = qt.shape[0], 4
     last = other is not None
     block = pl.BlockSpec((2, 256, 256), lambda s: (s, 0, 0))
@@ -255,7 +254,7 @@
     half = pl.BlockSpec((2, width, 256), lambda s: (s, chunk, 0))
     columns = pl.BlockSpec((2, 256, width), lambda s: (s, 0, chunk))
     in_specs = [pl.BlockSpec((512 * heads, 128), lambda s: (0, 0))]
-    in_specs += [half, half, half, columns, columns, half, half, half, block, block]
+    in_specs += [half, half, half, columns, columns, half, half, block, block]
     out_specs = [
         pl.BlockSpec((2, 4, width, 256), lambda s: (s, 0, 0, 0)),
         pl.BlockSpec((width, 128), lambda s: (0, 0)),
@@ -270,7 +269,7 @@
         pltpu.VMEM((512 * heads, 128), F32),
         pltpu.VMEM((5 * width, 256), F32),
     ]
-    operands = [bias, qt, kt, vt, k, v, gt, dgt, dat, xn, adj]
+    operands = [bias, qt, kt, vt, k, v, gt, dat, xn, adj]
     height = 8 * heads + (24 if last else 16)
     out_specs.append(pl.BlockSpec((64, height, 128), lambda s: (0, 0, 0)))
     out_shape.append(jax.ShapeDtypeStruct((64, height, 128), BF16))

time: 153 us -> 153 us (level)
  no operation moved by 1% of the time
where the time goes in v5:
time: 153 us; the launch traced here: 152 us
  Pallas kernels  47.4 us (31%)
  waiting for transfers between devices  37.4 us (24%)
  blocking collectives  32.2 us (21%)
  starting transfers between devices  29.4 us (19%)
  local copies, waits for them, and re-layouts  3.95 us (3%)
    all_to_all x6, waiting for transfers between devices, exchange(): return lax.all_to_all(blocks, axes, 0, 0, tiled=True)  35.3 us
    all_to_all x2, blocking collectives, exchange(): return lax.all_to_all(blocks, axes, 0, 0, tiled=True)  32.2 us
    all_to_all x6, starting transfers between devices, exchange(): return lax.all_to_all(blocks, axes, 0, 0, tiled=True)  27.4 us
    pallas_call x2, Pallas kernels, attend(): pl.pallas_call(kernel, grid=(rows // 2,), in_specs=in_specs, out_specs=ou...  24.6 us
    pallas_call x1, Pallas kernels, inputs_grad(): pl.pallas_call(kernel, grid=(rows,), in_specs=[block, whole(w), whole(gai...  8.55 us
    pallas_call x1, Pallas kernels, project(): pl.pallas_call(project_kernel, grid=(rows // 2,), in_specs=[block, block,...  7.88 us
  transfers between devices with their start and end apart: 9, of which 7 were waited for; matrix products, arithmetic and copies ran while one was open for 0% of the time, Pallas kernels for 29%

profile of v5, /device:TPU:2, one launch (start us, length us, event | category | flops | bytes accessed | tf_op | source)
XLA Modules:
  0.0 152.1 jit_solution(17434787075163283625)
XLA Ops:
  0.6 2.2 %pair_bias.1 = f32[8,64,128]{2,1,0:T(8,128)} custom-call(bf16[4,256,128]{2,1,0:T(8,128)(2,1)} %bitcast.20, f32[1,128]{1,0:T(1,128)} %bitcast.26, bf16[8,128]{1,0:T(8,128)(2,1)} %bitcast.23), custom_call_target="tpu_custom_call" | custom-call | flops 1000 | bytes 1000 | tf_op jit(solution)/shard_map/pair_bias/pallas_call | solution.py:418
  2.9 20.3 %all_to_all.40.column_ref = f32[8,64,128]{2,1,0:T(8,128)S(1)} all-to-all(f32[8,64,128]{2,1,0:T(8,128)} %pair_bias.1), channel_id=1, replica_groups=mesh['x_lo'=2,'core'=2,'y'=4,'z'=8,'x_hi'=2] {'z'}, dimensions={0} | all-to-all | bytes 524288 | tf_op jit(solution)/shard_map/all_to_all | solution.py:486
  23.2 0.0 copy-start.7
  23.2 1.1 broadcast_in_dim.10
  24.3 6.0 %all-to-all-start.1 = ((f32[8,8,32,128]{3,2,1,0:T(8,128)}), f32[8,8,32,128]{3,2,1,0:T(8,128)S(1)}, u32[]{:S(2)}, u32[]{:S(2)}) async-start(f32[8,8,32,128]{3,2,1,0:T(8,128)} %broadcast_in_dim.10), calls=%async_computation.1 | async-start | bytes 2097152 | tf_op jit(solution)/shard_map/all_to_all | solution.py:486
  30.3 0.0 copy-done.7
  30.3 7.9 %project.1 = (bf16[8,256,256]{2,1,0:T(8,128)(2,1)}, bf16[8,256,256]{2,1,0:T(8,128)(2,1)}, bf16[8,256,256]{2,1,0:T(8,128)(2,1)}, bf16[8,256,256]{2,1,0:T(8,128)(2...) custom-call(bf16[8,256,256]{2,1,0:T(8,128)(2,1)} %bitcast.33, ...), custom_call_target="tpu_custom_call" | custom-call | flops 1000 | bytes 1000 | tf_op jit(solution)/shard_map/project/pallas_call | solution.py:109
  38.2 7.6 %all-to-all-done.1 = f32[8,8,32,128]{3,2,1,0:T(8,128)S(1)} async-done(((f32[8,8,32,128]{3,2,1,0:T(8,128)}), f32[8,8,32,128]{3,2,1,0:T(8,128)S(1)}, u32[]{:S(2)}, u32[]{:S(2)}) %all-to-all-start.1) | async-done | bytes 1048608 | tf_op jit(solution)/shard_map/all_to_all | solution.py:486
  45.8 0.0 copy-start.6
  45.8 3.6 %all-to-all-start.2 = ((f32[8,256,128]{2,1,0:T(8,128)}), f32[8,256,128]{2,1,0:T(8,128)S(1)}, u32[]{:S(2)}, u32[]{:S(2)}) async-start(f32[8,256,128]{2,1,0:T(8,128)} %get-tuple-element.46), calls=%async_computation.2 | async-start | bytes 2097152 | tf_op jit(solution)/shard_map/all_to_all | solution.py:486
  49.4 0.0 copy-done.6
  49.4 12.2 %attend.2 = (bf16[8,4,128,256]{3,2,1,0:T(8,128)(2,1)}, f32[128,128]{1,0:T(8,128)}, bf16[64,48,128]{2,1,0:T(8,128)(2,1)}, f32[2,128,128]{2,1,0:T(8,128)}) custom-call(f32[2048,128]{1,0:T(8,128)} %bitcast.35, bf16[8,256,256]{2,1,0:T(8,128)(2,1)} %get-tuple-element.37.refs_1_, bf16[8,256,256]{2,1,0:T(8,128)(2,1)} %get-tuple-element.38.refs_2_, ...), custom_call_target="tpu_custom_call" | custom-call | flops 1000 | bytes 1000 | tf_op jit(solution)/shard_map/attend/pallas_call | solution.py:284
  61.6 2.6 %all-to-all-done.2 = f32[8,256,128]{2,1,0:T(8,128)S(1)} async-done(((f32[8,256,128]{2,1,0:T(8,128)}), f32[8,256,128]{2,1,0:T(8,128)S(1)}, u32[]{:S(2)}, u32[]{:S(2)}) %all-to-all-start.2) | async-done | bytes 1048608 | tf_op jit(solution)/shard_map/all_to_all | solution.py:486
  64.2 0.0 copy-start.5
  64.3 3.5 %all-to-all-start.3 = ((bf16[4,16,48,128]{3,2,1,0:T(8,128)(2,1)}), bf16[4,16,48,128]{3,2,1,0:T(8,128)(2,1)S(1)}, u32[]{:S(2)}, u32[]{:S(2)}) async-start(bf16[4,16,48,128]{3,2,1,0:T(8,128)(2,1)} %bitcast.37), calls=%async_computation.3 | async-start | bytes 1572864 | tf_op jit(solution)/shard_map/all_to_all | solution.py:486
  67.8 0.0 copy-done.5
  67.8 12.3 %attend.3 = (bf16[8,4,128,256]{3,2,1,0:T(8,128)(2,1)}, f32[128,128]{1,0:T(8,128)}, bf16[64,56,128]{2,1,0:T(8,128)(2,1)}) custom-call(f32[2048,128]{1,0:T(8,128)} %bitcast.32, bf16[8,256,256]{2,1,0:T(8,128)(2,1)} %get-tuple-element.37.refs_1_, bf16[8,256,256]{2,1,0:T(8,128)(2,1)} %get-tuple-element.38.refs_2_, ...), custom_call_target="tpu_custom_call" | custom-call | flops 1000 | bytes 1000 | tf_op jit(solution)/shard_map/attend/pallas_call | solution.py:284
  80.1 0.0 all-to-all-done.3
  80.1 4.7 %all-to-all-start.4 = ((bf16[4,16,56,128]{3,2,1,0:T(8,128)(2,1)}), bf16[4,16,56,128]{3,2,1,0:T(8,128)(2,1)S(1)}, u32[]{:S(2)}, u32[]{:S(2)}) async-start(bf16[4,16,56,128]{3,2,1,0:T(8,128)(2,1)} %bitcast.36), calls=%async_computation.4 | async-start | bytes 1835008 | tf_op jit(solution)/shard_map/all_to_all | solution.py:486
  84.8 0.1 reduce_sum.36
  85.0 10.0 %all-to-all-done.4 = bf16[4,16,56,128]{3,2,1,0:T(8,128)(2,1)S(1)} async-done(((bf16[4,16,56,128]{3,2,1,0:T(8,128)(2,1)}), bf16[4,16,56,128]{3,2,1,0:T(8,128)(2,1)S(1)}, u32[]{:S(2)}, u32[]{:S(2)}) %all-to-all-start.4) | async-done | bytes 917536 | tf_op jit(solution)/shard_map/all_to_all | solution.py:486
  95.0 0.1 reduce_sum.37
  95.2 0.8 pad_maximum_fusion
  96.0 5.7 %all-to-all-start.5 = ((bf16[16,104,128]{2,1,0:T(8,128)(2,1)}), bf16[16,104,128]{2,1,0:T(8,128)(2,1)S(1)}, u32[]{:S(2)}, u32[]{:S(2)}) async-start(bf16[16,104,128]{2,1,0:T(8,128)(2,1)} %pad_maximum_fusion), calls=%async_computation.5 | async-start | bytes 851968 | tf_op jit(solution)/shard_map/all_to_all | solution.py:486
  101.7 0.0 copy-start.2
  101.7 8.6 %inputs_grad.1 = (bf16[8,256,256]{2,1,0:T(8,128)(2,1)}, f32[8,128]{1,0:T(8,128)}, bf16[1024,384]{1,0:T(8,128)(2,1)}) custom-call(bf16[8,256,256]{2,1,0:T(8,128)(2,1)} %bitcast.34, bf16[256,1024]{1,0:T(8,128)(2,1)} %refs_1_.1, f32[1,256]{1,0:T(1,128)} %bitcast.41, bf16[8,4,128,256]{3,2,1,0:T(8,128)(2,1)} %get-tuple-element.45.refs_3_, ...), custom_call_target="tpu_custom_call" | custom-call | flops 1000 | bytes 1000 | tf_op jit(solution)/shard_map/inputs_grad/pallas_call | solution.py:343
  110.2 5.2 %all-to-all-done.5.parts_ref = bf16[16,104,128]{2,1,0:T(8,128)(2,1)S(1)} async-done(((bf16[16,104,128]{2,1,0:T(8,128)(2,1)}), bf16[16,104,128]{2,1,0:T(8,128)(2,1)S(1)}, u32[]{:S(2)}, u32[]{:S(2)}) %all-to-all-start.5) | async-done | bytes 426016 | tf_op jit(solution)/shard_map/all_to_all | solution.py:486
  115.4 0.0 copy-done.2
  115.4 0.0 copy-start.1
  115.4 1.1 copy-done.1
  116.6 0.0 copy-start.4
  116.6 0.7 copy-done.4
  117.2 0.0 copy-start
  117.2 0.0 copy-start.3
  117.2 0.3 pair_sums.1
  117.5 0.1 collective-permute-start.2
  117.6 1.5 collective-permute-start.1
  119.1 0.3 collective-permute-start
  119.5 1.7 %collective-permute-done.2 = f32[56,128]{1,0:T(8,128)S(1)} collective-permute-done((f32[56,128]{1,0:T(8,128)S(1)}, f32[56,128]{1,0:T(8,128)S(1)}, u32[]{:S(2)}, u32[]{:S(2)}) %collective-permute-start.2) | collective-permute-done | bytes 28704 | tf_op jit(solution)/shard_map/ppermute | solution.py:514
  121.2 0.4 collective-permute-done.1
  121.6 0.0 collective-permute-done
  121.6 11.8 %all_to_all.41 = bf16[8,56,128]{2,1,0:T(8,128)(2,1)S(1)} all-to-all(bf16[8,56,128]{2,1,0:T(8,128)(2,1)S(1)} %broadcast_in_dim.13), channel_id=1, replica_groups=mesh['x_lo'=2,'core'=2,'y'=4,'z'=8,'x_hi'=2] {'z'}, dimensions={0} | all-to-all | bytes 229376 | tf_op jit(solution)/shard_map/all_to_all | solution.py:486
  133.5 0.9 broadcast_in_dim.28
  134.4 4.0 %all-to-all-start.7 = ((bf16[8,336,128]{2,1,0:T(8,128)(2,1)}), bf16[8,336,128]{2,1,0:T(8,128)(2,1)S(1)}, u32[]{:S(2)}, u32[]{:S(2)}) async-start(bf16[8,336,128]{2,1,0:T(8,128)(2,1)} %broadcast_in_dim.28), calls=%async_computation.7 | async-start | bytes 1376256 | tf_op jit(solution)/shard_map/all_to_all | solution.py:486
  138.4 0.0 copy-done
  138.4 0.0 copy-done.3
  138.4 2.6 %pair_grad.1 = bf16[4,256,128]{2,1,0:T(8,128)(2,1)} custom-call(f32[64,128]{1,0:T(8,128)S(1)} %get-tuple-element.56.mine_ref, bf16[4,256,128]{2,1,0:T(8,128)(2,1)S(1)} %bitcast.22, f32[1,128]{1,0:T(1,128)S(1)} %bitcast.28, bf16[8,128]{1,0:T(8,128)(2,1)S(1)} %bitcast.25), custom_call_target="tpu_custom_call" | custom-call | flops 1000 | bytes 1000 | tf_op jit(solution)/shard_map/pair_grad/pallas_call | solution.py:476
  140.9 9.8 %all-to-all-done.7.total_ref = bf16[8,336,128]{2,1,0:T(8,128)(2,1)S(1)} async-done(((bf16[8,336,128]{2,1,0:T(8,128)(2,1)}), bf16[8,336,128]{2,1,0:T(8,128)(2,1)S(1)}, u32[]{:S(2)}, u32[]{:S(2)}) %all-to-all-start.7) | async-done | bytes 688160 | tf_op jit(solution)/shard_map/all_to_all | solution.py:486
  150.8 1.4 unpack.1
  (10 shorter events, 0.1 us)
Async XLA Ops:
  23.2 7.1 %copy-start.7 = (f32[8,64,128]{2,1,0:T(8,128)}, f32[8,64,128]{2,1,0:T(8,128)S(1)}, u32[]{:S(2)}) copy-start(f32[8,64,128]{2,1,0:T(8,128)S(1)} %all_to_all.40.column_ref) | copy-start | bytes 786436
  24.3 21.5 %all-to-all-start.1 = ((f32[8,8,32,128]{3,2,1,0:T(8,128)}), f32[8,8,32,128]{3,2,1,0:T(8,128)S(1)}, u32[]{:S(2)}, u32[]{:S(2)}) async-start(f32[8,8,32,128]{3,2,1,0:T(8,128)} %broadcast_in_dim.10), calls=%async_computation.1 | async-start | bytes 2097152 | tf_op jit(solution)/shard_map/all_to_all | solution.py:486
  45.8 3.6 %copy-start.6 = (f32[8,8,32,128]{3,2,1,0:T(8,128)}, f32[8,8,32,128]{3,2,1,0:T(8,128)S(1)}, u32[]{:S(2)}) copy-start(f32[8,8,32,128]{3,2,1,0:T(8,128)S(1)} %all-to-all-done.1) | copy-start | bytes 3145732
  45.8 18.4 %all-to-all-start.2 = ((f32[8,256,128]{2,1,0:T(8,128)}), f32[8,256,128]{2,1,0:T(8,128)S(1)}, u32[]{:S(2)}, u32[]{:S(2)}) async-start(f32[8,256,128]{2,1,0:T(8,128)} %get-tuple-element.46), calls=%async_computation.2 | async-start | bytes 2097152 | tf_op jit(solution)/shard_map/all_to_all | solution.py:486
  64.2 3.5 %copy-start.5 = (f32[8,256,128]{2,1,0:T(8,128)}, f32[8,256,128]{2,1,0:T(8,128)S(1)}, u32[]{:S(2)}) copy-start(f32[8,256,128]{2,1,0:T(8,128)S(1)} %all-to-all-done.2) | copy-start | bytes 3145732
  64.3 15.9 %all-to-all-start.3 = ((bf16[4,16,48,128]{3,2,1,0:T(8,128)(2,1)}), bf16[4,16,48,128]{3,2,1,0:T(8,128)(2,1)S(1)}, u32[]{:S(2)}, u32[]{:S(2)}) async-start(bf16[4,16,48,128]{3,2,1,0:T(8,128)(2,1)} %bitcast.37), calls=%async_computation.3 | async-start | bytes 1572864 | tf_op jit(solution)/shard_map/all_to_all | solution.py:486
  80.1 14.9 %all-to-all-start.4 = ((bf16[4,16,56,128]{3,2,1,0:T(8,128)(2,1)}), bf16[4,16,56,128]{3,2,1,0:T(8,128)(2,1)S(1)}, u32[]{:S(2)}, u32[]{:S(2)}) async-start(bf16[4,16,56,128]{3,2,1,0:T(8,128)(2,1)} %bitcast.36), calls=%async_computation.4 | async-start | bytes 1835008 | tf_op jit(solution)/shard_map/all_to_all | solution.py:486
  96.0 19.4 %all-to-all-start.5 = ((bf16[16,104,128]{2,1,0:T(8,128)(2,1)}), bf16[16,104,128]{2,1,0:T(8,128)(2,1)S(1)}, u32[]{:S(2)}, u32[]{:S(2)}) async-start(bf16[16,104,128]{2,1,0:T(8,128)(2,1)} %pad_maximum_fusion), calls=%async_computation.5 | async-start | bytes 851968 | tf_op jit(solution)/shard_map/all_to_all | solution.py:486
  101.7 13.7 %copy-start.2 = (bf16[128,8]{0,1:T(8,128)(2,1)S(1)}, bf16[128,8]{0,1:T(8,128)(2,1)}, u32[]{:S(2)}) copy-start(bf16[128,8]{0,1:T(8,128)(2,1)} %param.19) | copy-start | bytes 6148
  115.4 1.1 copy-start.1
  116.6 0.7 copy-start.4
  117.2 21.1 %copy-start = (bf16[1,4,256,128]{3,2,1,0:T(8,128)(2,1)S(1)}, bf16[1,4,256,128]{3,2,1,0:T(8,128)(2,1)}, u32[]{:S(2)}) copy-start(bf16[1,4,256,128]{3,2,1,0:T(8,128)(2,1)} %param.11) | copy-start | bytes 786436
  117.2 21.1 %copy-start.3 = (f32[128]{0:T(128)S(1)}, f32[128]{0:T(128)}, u32[]{:S(2)}) copy-start(f32[128]{0:T(128)} %param.18) | copy-start | bytes 1540
  117.5 3.7 %collective-permute-start.2 = (f32[56,128]{1,0:T(8,128)S(1)}, f32[56,128]{1,0:T(8,128)S(1)}, u32[]{:S(2)}, u32[]{:S(2)}) collective-permute-start(f32[56,128]{1,0:T(8,128)S(1)} %get-tuple-element.57), channel_id=1, source_target_pairs={{0,192},{64,128},{128,64},{192,0},{1,193},{65,129},{129,65},{193,1... | collective-permute-start | bytes 86024 | tf_op jit(solution)/shard_map/ppermute | solution.py:514
  117.6 4.0 %collective-permute-start.1 = (f32[56,128]{1,0:T(8,128)S(1)}, f32[56,128]{1,0:T(8,128)S(1)}, u32[]{:S(2)}, u32[]{:S(2)}) collective-permute-start(f32[56,128]{1,0:T(8,128)S(1)} %get-tuple-element.57), channel_id=1, source_target_pairs={{0,128},{64,192},{128,0},{192,64},{1,129},{65,193},{129,1},{193,65... | collective-permute-start | bytes 86024 | tf_op jit(solution)/shard_map/ppermute | solution.py:514
  119.1 2.4 %collective-permute-start = (f32[56,128]{1,0:T(8,128)S(1)}, f32[56,128]{1,0:T(8,128)S(1)}, u32[]{:S(2)}, u32[]{:S(2)}) collective-permute-start(f32[56,128]{1,0:T(8,128)S(1)} %get-tuple-element.57), channel_id=1, source_target_pairs={{0,64},{64,0},{128,192},{192,128},{1,65},{65,1},{129,193},{193,129... | collective-permute-start | bytes 86024 | tf_op jit(solution)/shard_map/ppermute | solution.py:514
  134.4 16.4 %all-to-all-start.7 = ((bf16[8,336,128]{2,1,0:T(8,128)(2,1)}), bf16[8,336,128]{2,1,0:T(8,128)(2,1)S(1)}, u32[]{:S(2)}, u32[]{:S(2)}) async-start(bf16[8,336,128]{2,1,0:T(8,128)(2,1)} %broadcast_in_dim.28), calls=%async_computation.7 | async-start | bytes 1376256 | tf_op jit(solution)/shard_map/all_to_all | solution.py:486
